TPU v7x, 32 devices: a whole 2x2x4 slice. The times are simulated.
32 devices in a mesh: tm: 8 (over z, y), space: 4 (over x, core).
Axes of the slice: x: 2, y: 2, z: 4, core: 2. Of those that a mesh axis runs over, the one named last changes fastest.
Arguments:
- start_states: float32 [8, 3, 16, 64, 256], P('tm', None, None, 'space'), may hold values from -6 to 6
- labels: int32 [16, 64, 256], P(None, 'space'), may hold values 0 or 1
Outputs:
- next_states: float32 [8, 3, 16, 64, 256], P('tm', None, None, 'space')
All inputs are finite; a program needn't handle non-finite values. No bound on the sum of `labels` on one device may be relied on, other than what follows from the above.
Results may differ from a plain program's by a relative error of at most 0.0001.
Values sent between devices are 32-bit elements; how exact they have to be, the bound alone decides.
A program may use at most 128 MiB of HBM per device.

v0:
```python
import jax
import jax.numpy as jnp
from jax import lax
from jax.sharding import PartitionSpec as P

VCYCLES = 2
COARSE_SWEEPS = 4


viscosity = 0.1
buoyancy = 0.2
relaxation = 0.8
coarse_rate = 0.15


def with_halo(cells, sides, width):
    for axis, dim in sides:
        count = lax.axis_size(axis)
        ends = count - 1
        head = lax.slice_in_dim(cells, 0, width, axis=dim)
        tail = lax.slice_in_dim(cells, cells.shape[dim] - width, cells.shape[dim], axis=dim)
        cells = jnp.concatenate(
            [
                lax.ppermute(tail, axis, [(i, (i + 1) % count) for i in range(ends)]),
                cells,
                lax.ppermute(head, axis, [((i + 1) % count, i) for i in range(ends)]),
            ],
            axis=dim,
        )
    return cells


def passed_along(shard, axis, by):
    peers = lax.axis_size(axis)
    pairs = [(i, i + by) for i in range(peers) if 0 <= i + by < peers]
    return lax.ppermute(shard, axis, pairs)


def neighbour(values, direction, offset):
    position = values.ndim + direction
    padding = [(0, 0)] * values.ndim
    padding[position] = (1, 1)
    padded = jnp.pad(values, padding)
    length = values.shape[position]
    return lax.slice_in_dim(padded, 1 + offset, 1 + offset + length, axis=position)


def restrict(values):
    leading = values.shape[:-3]
    depth_cells, across_cells, height_cells = values.shape[-3:]
    shaped = values.reshape(
        leading + (depth_cells // 2, 2, across_cells // 2, 2, height_cells // 2, 2)
    )
    return jnp.mean(shaped, axis=(-5, -3, -1))


def prolong(values):
    return jnp.repeat(jnp.repeat(jnp.repeat(values, 2, axis=-3), 2, axis=-2), 2, axis=-1)


def laplace_with(values, upper_across, lower_across):
    summed = neighbour(values, -3, 1) + neighbour(values, -3, -1) + upper_across + lower_across
    summed = summed + neighbour(values, -1, 1) + neighbour(values, -1, -1)
    return summed - 6.0 * values


def laplace(values):
    return laplace_with(values, neighbour(values, -2, 1), neighbour(values, -2, -1))


def face_weights(mobility, upper_across, lower_across):
    return (
        (
            0.5 * (mobility + neighbour(mobility, -3, 1)),
            0.5 * (mobility + neighbour(mobility, -3, -1)),
        ),
        (0.5 * (mobility + upper_across), 0.5 * (mobility + lower_across)),
        (
            0.5 * (mobility + neighbour(mobility, -1, 1)),
            0.5 * (mobility + neighbour(mobility, -1, -1)),
        ),
    )


def scaled_weights(weights):
    return tuple(((0.25 * upper_face, 0.25 * lower_face) for upper_face, lower_face in weights))


def weight_sum(weights):
    summed = weights[0][0] + weights[0][1]
    for upper_face, lower_face in weights[1:]:
        summed = summed + upper_face + lower_face
    return summed


def apply_weights(values, upper_across, lower_across, weights):
    depth_pair, across_pair, height_pair = weights
    summed = depth_pair[0] * (values - neighbour(values, -3, 1)) + depth_pair[1] * (
        values - neighbour(values, -3, -1)
    )
    summed = (
        summed + across_pair[0] * (values - upper_across) + across_pair[1] * (values - lower_across)
    )
    return (
        summed
        + height_pair[0] * (values - neighbour(values, -1, 1))
        + height_pair[1] * (values - neighbour(values, -1, -1))
    )


def pressure_sides(values):
    widened = with_halo(values, (("space", 1),), 1)
    extent = values.shape[1]
    return (widened[:, 2 : 2 + extent], widened[:, :extent])


def fine_operate(values, weights):
    upper_side, lower_side = pressure_sides(values)
    return apply_weights(values, upper_side, lower_side, weights)


def coarse_step(values, mobility_coarse):
    for substep in range(2):
        values = values + coarse_rate * mobility_coarse * laplace(values)
    return values


def body(start_states, labels):
    initial = start_states[0]
    mobility = 1.0 / (1.0 + 3.0 * labels.astype(jnp.float32))
    extent = mobility.shape[1]
    coarse_extent = extent // 2
    mobility_wide = with_halo(mobility, (("space", 1),), 8)
    weights = face_weights(
        mobility, mobility_wide[:, 9 : 9 + extent], mobility_wide[:, 7 : 7 + extent]
    )
    diagonal = weight_sum(weights)
    coarse_wide = restrict(mobility_wide)
    mobility_coarse = coarse_wide[:, 4 : 4 + coarse_extent]
    coarse_weights = scaled_weights(
        face_weights(
            mobility_coarse,
            coarse_wide[:, 5 : 5 + coarse_extent],
            coarse_wide[:, 3 : 3 + coarse_extent],
        )
    )
    coarse_diagonal = weight_sum(coarse_weights)
    velocity_wide = with_halo(initial, (("space", 2),), 1)
    zeros_field = jnp.zeros_like(mobility)
    predicted = initial + viscosity * laplace_with(
        initial, velocity_wide[:, :, 2 : 2 + extent], velocity_wide[:, :, :extent]
    )
    predicted = predicted + jnp.stack([buoyancy * (2.0 * mobility - 1.0), zeros_field, zeros_field])
    flux_wide = with_halo(predicted[1], (("space", 1),), 1)
    spread = (
        neighbour(predicted[0], -3, 1)
        - neighbour(predicted[0], -3, -1)
        + (flux_wide[:, 2 : 2 + extent] - flux_wide[:, :extent])
    )
    spread = spread + (neighbour(predicted[2], -1, 1) - neighbour(predicted[2], -1, -1))
    target = -0.5 * spread
    pressure = relaxation * target / diagonal
    for cycle_number in range(VCYCLES):
        if cycle_number > 0:
            pressure = pressure + relaxation * (target - fine_operate(pressure, weights)) / diagonal
        leftover = restrict(target - fine_operate(pressure, weights))
        correction = relaxation * leftover / coarse_diagonal
        for sweep_number in range(COARSE_SWEEPS - 1):
            widened = with_halo(correction, (("space", 1),), 1)
            applied = apply_weights(
                correction,
                widened[:, 2 : 2 + coarse_extent],
                widened[:, :coarse_extent],
                coarse_weights,
            )
            correction = correction + relaxation * (leftover - applied) / coarse_diagonal
        pressure = pressure + prolong(correction)
        pressure = pressure + relaxation * (target - fine_operate(pressure, weights)) / diagonal
    upper_side, lower_side = pressure_sides(pressure)
    gradient = jnp.stack(
        [
            0.5 * (neighbour(pressure, -3, 1) - neighbour(pressure, -3, -1)),
            0.5 * (upper_side - lower_side),
            0.5 * (neighbour(pressure, -1, 1) - neighbour(pressure, -1, -1)),
        ]
    )
    ending = predicted - mobility * gradient
    coarse_start = restrict(initial)
    coarse_end = restrict(ending)
    first_device = lax.axis_index("tm") == 0
    source, coarse_ends, mobility_all = (
        lax.all_gather(coarse_start, "space", axis=2, tiled=True),
        lax.all_gather(coarse_end, "space", axis=2, tiled=True),
        lax.all_gather(mobility_coarse, "space", axis=1, tiled=True),
    )
    partial_sum = jnp.where(
        first_device, coarse_ends, coarse_ends - coarse_step(source, mobility_all)
    )
    span = 1
    while span < lax.axis_size("tm"):
        received = passed_along(partial_sum, "tm", span)
        for repeat_number in range(span):
            received = coarse_step(received, mobility_all)
        partial_sum = partial_sum + received
        span = span * 2
    final_state = lax.dynamic_slice_in_dim(
        partial_sum, lax.axis_index("space") * coarse_extent, coarse_extent, 2
    )
    corrected = ending + prolong(final_state - coarse_end)
    return corrected[None]


def solution(mesh):
    in_specs = (P("tm", None, None, "space", None), P(None, "space", None))
    out_specs = P("tm", None, None, "space", None)
    return jax.shard_map(body, mesh=mesh, in_specs=in_specs, out_specs=out_specs, check_vma=False)
```

profile of v0, /device:TPU:25, one launch (start us, length us, event | category | flops | bytes accessed | tf_op | source)
XLA Modules:
  0.0 458.4 jit_solution(6366975728503843554)
XLA Ops:
  9.8 3.6 collective-permute-start.5
  13.6 4.5 fusion.8
  20.2 3.6 collective-permute-start.3
  27.2 4.2 collective-permute-start.7
  31.4 34.9 %reshape.42 = f32[8,2,16,2,128,2]{5,4,3,2,1,0:T(8,128)} reshape(f32[16,32,256]{2,1,0:T(8,128)S(1)} %pad_maximum_fusion.2) | data formatting | bytes 1048576 | tf_op jit(solution)/shard_map/reshape | solution.py:51
  66.3 12.2 %reduce_sum.46 = f32[8,16,128]{2,1,0:T(8,128)S(1)} reduce(f32[8,2,16,2,128,2]{5,4,3,2,1,0:T(8,128)} %reshape.42, f32[]{:T(128)} %constant.20.clone.1), dimensions={1,3,5}, to_apply=%region_1.2 | reduce | flops 114688 | bytes 589828 | tf_op jit(solution)/shard_map/reduce_sum | solution.py:54
  78.9 18.1 %reshape.41 = f32[8,2,8,2,128,2]{5,4,3,2,1,0:T(8,128)} reshape(f32[16,16,256]{2,1,0:T(8,128)S(1)} %fusion.149) | data formatting | bytes 524288 | tf_op jit(solution)/shard_map/reshape | solution.py:51
  97.0 7.0 %reduce_sum.45 = f32[8,8,128]{2,1,0:T(8,128)S(1)} reduce(f32[8,2,8,2,128,2]{5,4,3,2,1,0:T(8,128)} %reshape.41, f32[]{:T(128)} %constant.20.clone.1), dimensions={1,3,5}, to_apply=%region_0.1 | reduce | flops 57344 | bytes 294916 | tf_op jit(solution)/shard_map/reduce_sum | solution.py:54
  106.0 3.6 collective-permute-start.9
  112.5 4.2 collective-permute-start.11
  119.4 4.2 collective-permute-start.13
  136.4 4.2 collective-permute-start.15
  143.9 4.2 collective-permute-start.17
  151.9 4.4 collective-permute-start.19
  156.3 51.6 %reshape_squeeze.3 = f32[3,8,2,8,2,128,2]{6,5,4,3,2,1,0:T(8,128)} reshape(f32[1,3,16,16,256]{4,3,2,1,0:T(8,128)S(1)} %copy-done) | data formatting | bytes 1572864 | tf_op jit(solution)/shard_map/reshape;squeeze | solution.py:51
  208.0 18.4 %reduce_sum.49 = f32[3,8,8,128]{3,2,1,0:T(8,128)} reduce(f32[3,8,2,8,2,128,2]{6,5,4,3,2,1,0:T(8,128)} %reshape_squeeze.3, f32[]{:T(128)} %constant.20.clone.1), dimensions={2,4,6}, to_apply=%region_4.5 | reduce | flops 172032 | bytes 884740 | tf_op jit(solution)/shard_map/reduce_sum | solution.py:54
  228.9 18.8 %reshape.46 = f32[8,2,8,2,128,2]{5,4,3,2,1,0:T(8,128)} reshape(f32[16,16,256]{2,1,0:T(8,128)} %fusion.185) | data formatting | bytes 524288 | tf_op jit(solution)/shard_map/reshape | solution.py:51
  247.7 7.6 %reduce_sum.47 = f32[8,8,128]{2,1,0:T(8,128)} reduce(f32[8,2,8,2,128,2]{5,4,3,2,1,0:T(8,128)} %reshape.46, f32[]{:T(128)} %constant.20.clone.1), dimensions={1,3,5}, to_apply=%region_2.3 | reduce | flops 57344 | bytes 294916 | tf_op jit(solution)/shard_map/reduce_sum | solution.py:54
  258.1 3.6 collective-permute-start.21
  265.5 4.0 collective-permute-start.23
  269.5 5.8 %all_gather.10 = f32[3,8,32,128]{3,2,1,0:T(8,128)} all-gather(f32[3,8,8,128]{3,2,1,0:T(8,128)S(1)} %broadcast_multiply_fusion.1), channel_id=1, replica_groups=mesh['tm'=8,'space'=4] {'space'}, dimensions={2}, use_global_device_ids=true | all-gather | bytes 491520 | tf_op jit(solution)/shard_map/all_gather | solution.py:192
  282.8 4.8 %all_gather.11 = f32[8,32,128]{2,0,1:T(8,128)} all-gather(f32[8,8,128]{2,0,1:T(8,128)S(1)} %copy.197), channel_id=1, replica_groups=mesh['tm'=8,'space'=4] {'space'}, dimensions={1}, use_global_device_ids=true | all-gather | bytes 163840 | tf_op jit(solution)/shard_map/all_gather | solution.py:194
  305.8 4.2 collective-permute-start.29
  310.0 3.7 fusion.17
  315.4 51.6 %reshape.50 = f32[3,8,2,8,2,128,2]{6,5,4,3,2,1,0:T(8,128)} reshape(f32[3,16,16,256]{3,2,1,0:T(8,128)S(1)} %fusion.9) | data formatting | bytes 1572864 | tf_op jit(solution)/shard_map/reshape | solution.py:51
  367.1 17.8 %reduce_sum.48 = f32[3,8,8,128]{3,2,1,0:T(8,128)S(1)} reduce(f32[3,8,2,8,2,128,2]{6,5,4,3,2,1,0:T(8,128)} %reshape.50, f32[]{:T(128)} %constant.20.clone.1), dimensions={2,4,6}, to_apply=%region_3.4 | reduce | flops 172032 | bytes 884740 | tf_op jit(solution)/shard_map/reduce_sum | solution.py:54
  384.9 5.4 %all_gather.9 = f32[3,8,32,128]{3,2,1,0:T(8,128)S(1)} all-gather(f32[3,8,8,128]{3,2,1,0:T(8,128)S(1)} %broadcast_multiply_fusion.2), channel_id=1, replica_groups=mesh['tm'=8,'space'=4] {'space'}, dimensions={2}, use_global_device_ids=true | all-gather | bytes 491520 | tf_op jit(solution)/shard_map/all_gather | solution.py:193
  394.0 9.8 %collective-permute-done.30 = f32[3,8,32,128]{3,2,1,0:T(8,128)S(1)} collective-permute-done((f32[3,8,32,128]{3,2,1,0:T(8,128)S(1)}, f32[3,8,32,128]{3,2,1,0:T(8,128)S(1)}, u32[]{:S(2)}, u32[]{:S(2)}) %collective-permute-start.30) | collective-permute-done | bytes 393248 | tf_op jit(solution)/shard_map/ppermute | solution.py:36
  405.6 10.0 %collective-permute-done.31 = f32[3,8,32,128]{3,2,1,0:T(8,128)S(1)} collective-permute-done((f32[3,8,32,128]{3,2,1,0:T(8,128)S(1)}, f32[3,8,32,128]{3,2,1,0:T(8,128)S(1)}, u32[]{:S(2)}, u32[]{:S(2)}) %collective-permute-start.31) | collective-permute-done | bytes 393248 | tf_op jit(solution)/shard_map/ppermute | solution.py:36
  418.1 20.9 %collective-permute-done.32 = f32[3,8,32,128]{3,2,1,0:T(8,128)} collective-permute-done((f32[3,8,32,128]{3,2,1,0:T(8,128)S(1)}, f32[3,8,32,128]{3,2,1,0:T(8,128)}, u32[]{:S(2)}, u32[]{:S(2)}) %collective-permute-start.32) | collective-permute-done | bytes 393248 | tf_op jit(solution)/shard_map/ppermute | solution.py:36
  446.7 5.1 %broadcast_in_dim.55 = f32[3,16,16,128,2]{2,1,4,3,0:T(8,128)} broadcast(f32[3,16,16,128]{2,1,3,0:T(8,128)} %copy.200), dimensions={0,1,2,3} | broadcast | bytes 1179648 | tf_op jit(solution)/shard_map/broadcast_in_dim | solution.py:58
  451.8 5.1 %copy.201 = f32[3,16,16,256]{3,2,1,0:T(8,128)S(1)} copy(f32[3,16,16,256]{2,1,3,0:T(8,128)} %bitcast.30) | data formatting | bytes 1572864 | tf_op jit(solution)/shard_map/reshape | solution.py:58
  (184 shorter events, 96.0 us)
Async XLA Ops:
  1.2 12.3 %collective-permute-start = (f32[3,16,1,256]{3,1,2,0:T(8,128)S(1)}, f32[3,16,1,256]{3,1,2,0:T(8,128)S(1)}, u32[]{:S(2)}, u32[]{:S(2)}) collective-permute-start(f32[3,16,1,256]{3,1,2,0:T(8,128)S(1)} %copy.159), channel_id=1, source_target_pairs={{1,0},{2,1},{3,2},{5,4},{6,5},{7,6},{9,8},{10,9},{11,10},{13,12},{... | collective-permute-start | bytes 147464 | tf_op jit(solution)/shard_map/ppermute | solution.py:26
  3.8 9.7 %collective-permute-start.1 = (f32[3,16,1,256]{3,1,2,0:T(8,128)S(1)}, f32[3,16,1,256]{3,1,2,0:T(8,128)S(1)}, u32[]{:S(2)}, u32[]{:S(2)}) collective-permute-start(f32[3,16,1,256]{3,1,2,0:T(8,128)S(1)} %copy.161), channel_id=1, source_target_pairs={{0,1},{1,2},{2,3},{4,5},{5,6},{6,7},{8,9},{9,10},{10,11},{12,13},{... | collective-permute-start | bytes 147464 | tf_op jit(solution)/shard_map/ppermute | solution.py:24
  7.9 16.8 %collective-permute-start.4 = (f32[16,8,256]{2,1,0:T(8,128)S(1)}, f32[16,8,256]{2,1,0:T(8,128)S(1)}, u32[]{:S(2)}, u32[]{:S(2)}) collective-permute-start(f32[16,8,256]{2,1,0:T(8,128)S(1)} %get-tuple-element.44), channel_id=1, source_target_pairs={{1,0},{2,1},{3,2},{5,4},{6,5},{7,6},{9,8},{10,9},{11,10},{13,12},{... | collective-permute-start | bytes 393224 | tf_op jit(solution)/shard_map/ppermute | solution.py:26
  9.8 14.9 %collective-permute-start.5 = (f32[16,8,256]{2,1,0:T(8,128)S(1)}, f32[16,8,256]{2,1,0:T(8,128)S(1)}, u32[]{:S(2)}, u32[]{:S(2)}) collective-permute-start(f32[16,8,256]{2,1,0:T(8,128)S(1)} %get-tuple-element.43), channel_id=1, source_target_pairs={{0,1},{1,2},{2,3},{4,5},{5,6},{6,7},{8,9},{9,10},{10,11},{12,13},{... | collective-permute-start | bytes 393224 | tf_op jit(solution)/shard_map/ppermute | solution.py:24
  18.3 5.6 %collective-permute-start.2 = (f32[16,1,256]{2,0,1:T(8,128)S(1)}, f32[16,1,256]{2,0,1:T(8,128)S(1)}, u32[]{:S(2)}, u32[]{:S(2)}) collective-permute-start(f32[16,1,256]{2,0,1:T(8,128)S(1)} %copy.163), channel_id=1, source_target_pairs={{1,0},{2,1},{3,2},{5,4},{6,5},{7,6},{9,8},{10,9},{11,10},{13,12},{... | collective-permute-start | bytes 49160 | tf_op jit(solution)/shard_map/ppermute | solution.py:26
  20.2 4.5 collective-permute-start.3
  25.2 53.3 %collective-permute-start.6 = (f32[16,1,256]{2,0,1:T(8,128)S(1)}, f32[16,1,256]{2,0,1:T(8,128)S(1)}, u32[]{:S(2)}, u32[]{:S(2)}) collective-permute-start(f32[16,1,256]{2,0,1:T(8,128)S(1)} %copy.167), channel_id=1, source_target_pairs={{1,0},{2,1},{3,2},{5,4},{6,5},{7,6},{9,8},{10,9},{11,10},{13,12},{... | collective-permute-start | bytes 49160 | tf_op jit(solution)/shard_map/ppermute | solution.py:26
  27.2 51.4 %collective-permute-start.7 = (f32[16,1,256]{2,0,1:T(8,128)S(1)}, f32[16,1,256]{2,0,1:T(8,128)S(1)}, u32[]{:S(2)}, u32[]{:S(2)}) collective-permute-start(f32[16,1,256]{2,0,1:T(8,128)S(1)} %copy.169), channel_id=1, source_target_pairs={{0,1},{1,2},{2,3},{4,5},{5,6},{6,7},{8,9},{9,10},{10,11},{12,13},{... | collective-permute-start | bytes 49160 | tf_op jit(solution)/shard_map/ppermute | solution.py:24
  104.1 5.6 %collective-permute-start.8 = (f32[8,1,128]{2,1,0:T(1,128)S(1)}, f32[8,1,128]{2,1,0:T(1,128)S(1)}, u32[]{:S(2)}, u32[]{:S(2)}) collective-permute-start(f32[8,1,128]{2,1,0:T(1,128)S(1)} %get-tuple-element.59), channel_id=1, source_target_pairs={{1,0},{2,1},{3,2},{5,4},{6,5},{7,6},{9,8},{10,9},{11,10},{13,12},{... | collective-permute-start | bytes 12296 | tf_op jit(solution)/shard_map/ppermute | solution.py:26
  106.0 4.4 collective-permute-start.9
  110.5 6.1 %collective-permute-start.10 = (f32[8,1,128]{2,1,0:T(1,128)S(1)}, f32[8,1,128]{2,1,0:T(1,128)S(1)}, u32[]{:S(2)}, u32[]{:S(2)}) collective-permute-start(f32[8,1,128]{2,1,0:T(1,128)S(1)} %get-tuple-element.57), channel_id=1, source_target_pairs={{1,0},{2,1},{3,2},{5,4},{6,5},{7,6},{9,8},{10,9},{11,10},{13,12},{... | collective-permute-start | bytes 12296 | tf_op jit(solution)/shard_map/ppermute | solution.py:26
  112.5 4.9 %collective-permute-start.11 = (f32[8,1,128]{2,1,0:T(1,128)S(1)}, f32[8,1,128]{2,1,0:T(1,128)S(1)}, u32[]{:S(2)}, u32[]{:S(2)}) collective-permute-start(f32[8,1,128]{2,1,0:T(1,128)S(1)} %get-tuple-element.58), channel_id=1, source_target_pairs={{0,1},{1,2},{2,3},{4,5},{5,6},{6,7},{8,9},{9,10},{10,11},{12,13},{... | collective-permute-start | bytes 12296 | tf_op jit(solution)/shard_map/ppermute | solution.py:24
  117.5 6.1 %collective-permute-start.12 = (f32[8,1,128]{2,1,0:T(1,128)S(1)}, f32[8,1,128]{2,1,0:T(1,128)S(1)}, u32[]{:S(2)}, u32[]{:S(2)}) collective-permute-start(f32[8,1,128]{2,1,0:T(1,128)S(1)} %get-tuple-element.55), channel_id=1, source_target_pairs={{1,0},{2,1},{3,2},{5,4},{6,5},{7,6},{9,8},{10,9},{11,10},{13,12},{... | collective-permute-start | bytes 12296 | tf_op jit(solution)/shard_map/ppermute | solution.py:26
  119.4 4.9 %collective-permute-start.13 = (f32[8,1,128]{2,1,0:T(1,128)S(1)}, f32[8,1,128]{2,1,0:T(1,128)S(1)}, u32[]{:S(2)}, u32[]{:S(2)}) collective-permute-start(f32[8,1,128]{2,1,0:T(1,128)S(1)} %get-tuple-element.56), channel_id=1, source_target_pairs={{0,1},{1,2},{2,3},{4,5},{5,6},{6,7},{8,9},{9,10},{10,11},{12,13},{... | collective-permute-start | bytes 12296 | tf_op jit(solution)/shard_map/ppermute | solution.py:24
  134.5 6.1 %collective-permute-start.14 = (f32[16,1,256]{2,0,1:T(8,128)S(1)}, f32[16,1,256]{2,0,1:T(8,128)S(1)}, u32[]{:S(2)}, u32[]{:S(2)}) collective-permute-start(f32[16,1,256]{2,0,1:T(8,128)S(1)} %copy.174), channel_id=1, source_target_pairs={{1,0},{2,1},{3,2},{5,4},{6,5},{7,6},{9,8},{10,9},{11,10},{13,12},{... | collective-permute-start | bytes 49160 | tf_op jit(solution)/shard_map/ppermute | solution.py:26
  136.4 5.0 %collective-permute-start.15 = (f32[16,1,256]{2,0,1:T(8,128)S(1)}, f32[16,1,256]{2,0,1:T(8,128)S(1)}, u32[]{:S(2)}, u32[]{:S(2)}) collective-permute-start(f32[16,1,256]{2,0,1:T(8,128)S(1)} %copy.176), channel_id=1, source_target_pairs={{0,1},{1,2},{2,3},{4,5},{5,6},{6,7},{8,9},{9,10},{10,11},{12,13},{... | collective-permute-start | bytes 49160 | tf_op jit(solution)/shard_map/ppermute | solution.py:24
  141.9 6.2 %collective-permute-start.16 = (f32[16,1,256]{2,0,1:T(8,128)S(1)}, f32[16,1,256]{2,0,1:T(8,128)S(1)}, u32[]{:S(2)}, u32[]{:S(2)}) collective-permute-start(f32[16,1,256]{2,0,1:T(8,128)S(1)} %copy.178), channel_id=1, source_target_pairs={{1,0},{2,1},{3,2},{5,4},{6,5},{7,6},{9,8},{10,9},{11,10},{13,12},{... | collective-permute-start | bytes 49160 | tf_op jit(solution)/shard_map/ppermute | solution.py:26
  143.9 5.1 %collective-permute-start.17 = (f32[16,1,256]{2,0,1:T(8,128)S(1)}, f32[16,1,256]{2,0,1:T(8,128)S(1)}, u32[]{:S(2)}, u32[]{:S(2)}) collective-permute-start(f32[16,1,256]{2,0,1:T(8,128)S(1)} %copy.180), channel_id=1, source_target_pairs={{0,1},{1,2},{2,3},{4,5},{5,6},{6,7},{8,9},{9,10},{10,11},{12,13},{... | collective-permute-start | bytes 49160 | tf_op jit(solution)/shard_map/ppermute | solution.py:24
  149.4 77.0 %collective-permute-start.18 = (f32[16,1,256]{2,0,1:T(8,128)S(1)}, f32[16,1,256]{2,0,1:T(8,128)}, u32[]{:S(2)}, u32[]{:S(2)}) collective-permute-start(f32[16,1,256]{2,0,1:T(8,128)S(1)} %copy.182), channel_id=1, source_target_pairs={{1,0},{2,1},{3,2},{5,4},{6,5},{7,6},{9,8},{10,9},{11,10},{13,12},{... | collective-permute-start | bytes 49160 | tf_op jit(solution)/shard_map/ppermute | solution.py:26
  151.9 75.2 %collective-permute-start.19 = (f32[16,1,256]{2,0,1:T(8,128)}, f32[16,1,256]{2,0,1:T(8,128)}, u32[]{:S(2)}, u32[]{:S(2)}) collective-permute-start(f32[16,1,256]{2,0,1:T(8,128)} %copy.184), channel_id=1, source_target_pairs={{0,1},{1,2},{2,3},{4,5},{5,6},{6,7},{8,9},{9,10},{10,11},{12,13},{... | collective-permute-start | bytes 49160 | tf_op jit(solution)/shard_map/ppermute | solution.py:24
  256.1 6.5 %collective-permute-start.20 = (f32[8,1,128]{2,1,0:T(1,128)S(1)}, f32[8,1,128]{2,1,0:T(1,128)S(1)}, u32[]{:S(2)}, u32[]{:S(2)}) collective-permute-start(f32[8,1,128]{2,1,0:T(1,128)S(1)} %get-tuple-element.53), channel_id=1, source_target_pairs={{1,0},{2,1},{3,2},{5,4},{6,5},{7,6},{9,8},{10,9},{11,10},{13,12},{... | collective-permute-start | bytes 12296 | tf_op jit(solution)/shard_map/ppermute | solution.py:26
  258.1 4.6 collective-permute-start.21
  263.5 12.6 %collective-permute-start.22 = (f32[8,1,128]{2,1,0:T(1,128)S(1)}, f32[8,1,128]{2,1,0:T(1,128)S(1)}, u32[]{:S(2)}, u32[]{:S(2)}) collective-permute-start(f32[8,1,128]{2,1,0:T(1,128)S(1)} %get-tuple-element.51), channel_id=1, source_target_pairs={{1,0},{2,1},{3,2},{5,4},{6,5},{7,6},{9,8},{10,9},{11,10},{13,12},{... | collective-permute-start | bytes 12296 | tf_op jit(solution)/shard_map/ppermute | solution.py:26
  265.5 10.6 %collective-permute-start.23 = (f32[8,1,128]{2,1,0:T(1,128)S(1)}, f32[8,1,128]{2,1,0:T(1,128)S(1)}, u32[]{:S(2)}, u32[]{:S(2)}) collective-permute-start(f32[8,1,128]{2,1,0:T(1,128)S(1)} %get-tuple-element.52), channel_id=1, source_target_pairs={{0,1},{1,2},{2,3},{4,5},{5,6},{6,7},{8,9},{9,10},{10,11},{12,13},{... | collective-permute-start | bytes 12296 | tf_op jit(solution)/shard_map/ppermute | solution.py:24
  277.2 10.4 %collective-permute-start.24 = (f32[8,1,128]{2,1,0:T(1,128)S(1)}, f32[8,1,128]{2,1,0:T(1,128)S(1)}, u32[]{:S(2)}, u32[]{:S(2)}) collective-permute-start(f32[8,1,128]{2,1,0:T(1,128)S(1)} %get-tuple-element.49), channel_id=1, source_target_pairs={{1,0},{2,1},{3,2},{5,4},{6,5},{7,6},{9,8},{10,9},{11,10},{13,12},{... | collective-permute-start | bytes 12296 | tf_op jit(solution)/shard_map/ppermute | solution.py:26
  279.5 8.1 %collective-permute-start.25 = (f32[8,1,128]{2,1,0:T(1,128)S(1)}, f32[8,1,128]{2,1,0:T(1,128)S(1)}, u32[]{:S(2)}, u32[]{:S(2)}) collective-permute-start(f32[8,1,128]{2,1,0:T(1,128)S(1)} %get-tuple-element.50), channel_id=1, source_target_pairs={{0,1},{1,2},{2,3},{4,5},{5,6},{6,7},{8,9},{9,10},{10,11},{12,13},{... | collective-permute-start | bytes 12296 | tf_op jit(solution)/shard_map/ppermute | solution.py:24
  297.0 5.7 %collective-permute-start.26 = (f32[16,1,256]{2,0,1:T(8,128)S(1)}, f32[16,1,256]{2,0,1:T(8,128)S(1)}, u32[]{:S(2)}, u32[]{:S(2)}) collective-permute-start(f32[16,1,256]{2,0,1:T(8,128)S(1)} %copy.189), channel_id=1, source_target_pairs={{1,0},{2,1},{3,2},{5,4},{6,5},{7,6},{9,8},{10,9},{11,10},{13,12},{... | collective-permute-start | bytes 49160 | tf_op jit(solution)/shard_map/ppermute | solution.py:26
  303.9 9.8 %collective-permute-start.28 = (f32[16,1,256]{2,0,1:T(8,128)S(1)}, f32[16,1,256]{2,0,1:T(8,128)S(1)}, u32[]{:S(2)}, u32[]{:S(2)}) collective-permute-start(f32[16,1,256]{2,0,1:T(8,128)S(1)} %copy.193), channel_id=1, source_target_pairs={{1,0},{2,1},{3,2},{5,4},{6,5},{7,6},{9,8},{10,9},{11,10},{13,12},{... | collective-permute-start | bytes 49160 | tf_op jit(solution)/shard_map/ppermute | solution.py:26
  305.8 7.9 %collective-permute-start.29 = (f32[16,1,256]{2,0,1:T(8,128)S(1)}, f32[16,1,256]{2,0,1:T(8,128)S(1)}, u32[]{:S(2)}, u32[]{:S(2)}) collective-permute-start(f32[16,1,256]{2,0,1:T(8,128)S(1)} %copy.195), channel_id=1, source_target_pairs={{0,1},{1,2},{2,3},{4,5},{5,6},{6,7},{8,9},{9,10},{10,11},{12,13},{... | collective-permute-start | bytes 49160 | tf_op jit(solution)/shard_map/ppermute | solution.py:24
  390.6 13.1 %collective-permute-start.30 = (f32[3,8,32,128]{3,2,1,0:T(8,128)S(1)}, f32[3,8,32,128]{3,2,1,0:T(8,128)S(1)}, u32[]{:S(2)}, u32[]{:S(2)}) collective-permute-start(f32[3,8,32,128]{3,2,1,0:T(8,128)S(1)} %subtract_select_fusion), channel_id=1, source_target_pairs={{0,4},{4,8},{8,12},{12,16},{16,20},{20,24},{24,28},{1,5},{5,9},{9,... | collective-permute-start | bytes 1179656 | tf_op jit(solution)/shard_map/ppermute | solution.py:36
  404.3 11.3 %collective-permute-start.31 = (f32[3,8,32,128]{3,2,1,0:T(8,128)S(1)}, f32[3,8,32,128]{3,2,1,0:T(8,128)S(1)}, u32[]{:S(2)}, u32[]{:S(2)}) collective-permute-start(f32[3,8,32,128]{3,2,1,0:T(8,128)S(1)} %fusion.42), channel_id=1, source_target_pairs={{0,8},{4,12},{8,16},{12,20},{16,24},{20,28},{1,9},{5,13},{9,17},{1... | collective-permute-start | bytes 1179656 | tf_op jit(solution)/shard_map/ppermute | solution.py:36
  416.8 22.2 %collective-permute-start.32 = (f32[3,8,32,128]{3,2,1,0:T(8,128)S(1)}, f32[3,8,32,128]{3,2,1,0:T(8,128)}, u32[]{:S(2)}, u32[]{:S(2)}) collective-permute-start(f32[3,8,32,128]{3,2,1,0:T(8,128)S(1)} %fusion.75), channel_id=1, source_target_pairs={{0,16},{4,20},{8,24},{12,28},{1,17},{5,21},{9,25},{13,29},{2,18},{... | collective-permute-start | bytes 1179656 | tf_op jit(solution)/shard_map/ppermute | solution.py:36
  (13 other events, 215.6 us)
where the time goes:
time: 461 us; the launch traced here: 458 us
  local copies, waits for them, and re-layouts  209 us (45%)
  starting transfers between devices  93.8 us (20%)
  other arithmetic  92.5 us (20%)
  waiting for transfers between devices  46.1 us (10%)
  blocking collectives  16 us (3%)
    reshape x4, local copies, waits for them, and re-layouts, restrict(): values.reshape(leading + (depth_cells // 2, 2, across_cells // 2, 2, heig...  123 us
    reduce_sum x5, other arithmetic, restrict(): return jnp.mean(shaped, axis=(-5, -3, -1))  63 us
    ppermute x15, starting transfers between devices, with_halo(): lax.ppermute(tail, axis, [(i, (i + 1) % count) for i in range(ends)])  57.8 us
    another operation x1, local copies, waits for them, and re-layouts, restrict(): values.reshape(leading + (depth_cells // 2, 2, across_cells // 2, 2, heig...  51.6 us
    ppermute x3, waiting for transfers between devices, passed_along(): return lax.ppermute(shard, axis, pairs)  40.7 us
    ppermute x15, starting transfers between devices, with_halo(): lax.ppermute(head, axis, [((i + 1) % count, i) for i in range(ends)])  30 us
    reshape x3, local copies, waits for them, and re-layouts, prolong(): jnp.repeat(jnp.repeat(jnp.repeat(values, 2, axis=-3), 2, axis=-2), 2, axi...  11.4 us
    broadcast_in_dim x3, local copies, waits for them, and re-layouts, prolong(): jnp.repeat(jnp.repeat(jnp.repeat(values, 2, axis=-3), 2, axis=-2), 2, axi...  10.6 us
  transfers between devices with their start and end apart: 33, of which 10 were waited for; matrix products, arithmetic and copies ran while one was open for 28% of the time, Pallas kernels for 0%

commit v1 on v0

v1 whole, which is shorter than its diff:
```python
import functools
import jax
import jax.numpy as jnp
from jax import lax
from jax.experimental import pallas as pl
from jax.experimental.pallas import tpu as pltpu
from jax.sharding import PartitionSpec as P

VISCOSITY = 0.1
BUOYANCY = 0.2
OMEGA = 0.8
RATE = 0.15
CYCLES = 2
SWEEPS = 4
H = 10
MESH = pl.DeviceIdType.MESH
f32 = jnp.float32


def split_dot(a, b):
    a1 = a.astype(jnp.bfloat16)
    rest = a - a1.astype(f32)
    a2 = rest.astype(jnp.bfloat16)
    a3 = (rest - a2.astype(f32)).astype(jnp.bfloat16)
    dot = functools.partial(jnp.dot, preferred_element_type=f32)
    return dot(a1, b) + (dot(a2, b) + dot(a3, b))


def shifts(v, zaxis, yaxis):
    nz, ny = v.shape[zaxis], v.shape[yaxis]
    return (
        pltpu.roll(v, nz - 1, zaxis),
        pltpu.roll(v, 1, zaxis),
        pltpu.roll(v, ny - 1, yaxis),
        pltpu.roll(v, 1, yaxis),
    )


def edge_masks(shape, zaxis, yaxis):
    z = lax.broadcasted_iota(jnp.int32, shape, zaxis)
    y = lax.broadcasted_iota(jnp.int32, shape, yaxis)
    return z < shape[zaxis] - 1, z > 0, y < shape[yaxis] - 1, y > 0


def masked_shifts(v, masks, zaxis, yaxis):
    return [jnp.where(m, s, 0.0) for m, s in zip(masks, shifts(v, zaxis, yaxis))]


def planes(lo, hi, fn, step=2):
    def some(k, carry):
        for j in range(step):
            fn(lo + k * step + j)
        return carry

    assert (hi - lo) % step == 0
    lax.fori_loop(0, (hi - lo) // step, some, 0)


def x_up(v):
    return jnp.concatenate([v[1:], jnp.zeros_like(v[:1])], axis=0)


def x_down(v):
    return jnp.concatenate([jnp.zeros_like(v[:1]), v[:-1]], axis=0)


def kernel(n, ntm, spans, u_in, m_in, out, u, m, pr, t, pa, pb, pc, rd, dg, wx, wzu, wzl, wyu, wyl,
           rs, rz, mc, cw, ce, mcw, csw, cew, gs, part, recv, wfin, down, dup,
           local_sem, us, ur, ms, mr, ts, tr, ps, pr_sem, mcs, mcr, css, csr, ces, cer, ss, sr, fs, fr):
    me, tm = lax.axis_index("space"), lax.axis_index("tm")
    X, Z, Y = u_in.shape[1:]
    Xc, Zc, Yc = X // 2, Z // 2, Y // 2
    HC = H // 2
    C = u_in.shape[0]
    has_left, has_right = me > 0, me < n - 1

    loads = [
        pltpu.make_async_copy(u_in, u.at[:, pl.ds(2, X)], local_sem.at[0]),
        pltpu.make_async_copy(m_in, m.at[pl.ds(H, X)], local_sem.at[1]),
    ]
    for c in loads:
        c.start()

    barrier = pltpu.get_barrier_semaphore()
    for k in range(1, n):
        pl.semaphore_signal(barrier, inc=1, device_id={"space": lax.rem(me + k, n)}, device_id_type=MESH)
    count = n - 1
    for s in spans:
        @pl.when(tm >= s)
        def _():
            pl.semaphore_signal(barrier, inc=1, device_id={"tm": tm - s}, device_id_type=MESH)

        @pl.when(tm + s < ntm)
        def _():
            pl.semaphore_signal(barrier, inc=1, device_id={"tm": tm + s}, device_id_type=MESH)

        count = count + jnp.where(tm >= s, 1, 0) + jnp.where(tm + s < ntm, 1, 0)

    @pl.when(jnp.logical_not(has_left))
    def _():
        u[:, 0:2] = jnp.zeros((C, 2, Z, Y), f32)
        for ref in (m, t, pb):
            ref[0:H] = jnp.zeros((H, Z, Y), f32)

    @pl.when(jnp.logical_not(has_right))
    def _():
        u[:, X + 2:X + 4] = jnp.zeros((C, 2, Z, Y), f32)
        for ref in (m, t, pb):
            ref[X + H:X + 2 * H] = jnp.zeros((H, Z, Y), f32)

    row = lax.broadcasted_iota(jnp.int32, (Y, Yc), 0)
    col = lax.broadcasted_iota(jnp.int32, (Y, Yc), 1)
    down[...] = jnp.where(lax.div(row, 2) == col, 0.125, 0.0).astype(jnp.bfloat16)
    row = lax.broadcasted_iota(jnp.int32, (Yc, Y), 0)
    col = lax.broadcasted_iota(jnp.int32, (Yc, Y), 1)
    dup[...] = jnp.where(row == lax.div(col, 2), 1.0, 0.0).astype(jnp.bfloat16)

    def restricted(count_c, plane_sum):
        def one(j, carry):
            rs[pl.ds(pl.multiple_of(j * Z, Z), Z), :] = plane_sum(j)
            return carry

        lax.fori_loop(0, count_c, one, 0)
        rows = count_c * Z
        rz[0:rows, :] = split_dot(rs[0:rows, :], down[...])
        half = rows // 2
        return (rz[pl.ds(0, half, stride=2), :] + rz[pl.ds(1, half, stride=2), :]).reshape(count_c, Zc, Yc)

    def prolonged(v):
        half = v.shape[0] * Zc
        flat = v.reshape(half, Yc)
        rz[pl.ds(0, half, stride=2), :] = flat
        rz[pl.ds(1, half, stride=2), :] = flat
        rs[0:2 * half, :] = split_dot(rz[0:2 * half, :], dup[...])

    def to_left(src, dst, ssem, rsem):
        return pltpu.make_async_remote_copy(src, dst, ssem, rsem, device_id={"space": me - 1}, device_id_type=MESH)

    def to_right(src, dst, ssem, rsem):
        return pltpu.make_async_remote_copy(src, dst, ssem, rsem, device_id={"space": me + 1}, device_id_type=MESH)

    class Exchange:
        def __init__(self, items, ssem, rsem):
            self.left, self.right = [], []
            for k, (at, first, width) in enumerate(items):
                self.left.append(to_left(at(first, width), at(first + X, width), ssem.at[0, k], rsem.at[0, k]))
                self.right.append(
                    to_right(at(first + X - width, width), at(first - width, width), ssem.at[1, k], rsem.at[1, k]))

        def start(self):
            @pl.when(has_left)
            def _():
                for c in self.left:
                    c.start()

            @pl.when(has_right)
            def _():
                for c in self.right:
                    c.start()

        def wait(self):
            @pl.when(has_left)
            def _():
                for c in self.left:
                    c.wait_send()
                for c in self.right:
                    c.wait_recv()

            @pl.when(has_right)
            def _():
                for c in self.right:
                    c.wait_send()
                for c in self.left:
                    c.wait_recv()

    def plane_view(ref):
        return lambda first, width: ref.at[pl.ds(first, width)]

    for c in loads:
        c.wait()
    pl.semaphore_wait(barrier, count)

    u_x = Exchange([(lambda f, w, d=d: u.at[d, pl.ds(f, w)], 2, 2 if d == 1 else 1) for d in range(C)], us, ur)
    m_x = Exchange([(plane_view(m), H, H)], ms, mr)
    t_x = Exchange([(plane_view(t), H, H - 1)], ts, tr)
    p_x = Exchange([(plane_view(pb), H, H)], ps, pr_sem)
    u_x.start()
    m_x.start()

    def own_rows(ref):
        return ref.at[pl.ds(me * Xc, Xc)]

    mine = restricted(Xc, lambda j: m[H + 2 * j] + m[H + 2 * j + 1])
    mc[HC:HC + Xc] = mine
    mcw[pl.ds(me * Xc, Xc)] = mine
    for d in range(C):
        gs[d] = restricted(Xc, lambda j: u[d, 2 + 2 * j] + u[d, 3 + 2 * j])

    def mc_copy(k, src):
        peer = lax.rem(me + k, n)
        at = mc.at[pl.ds(HC, Xc)]
        return pltpu.make_async_remote_copy(
            at, mcw.at[pl.ds(src * Xc, Xc)], mcs.at[k], mcr.at[k], device_id={"space": peer}, device_id_type=MESH)

    for k in range(1, n):
        mc_copy(k, me).start()

    def gather_copy(src, dst, d, ssem, rsem, sender):
        return pltpu.make_async_remote_copy(
            src.at[d], dst.at[pl.ds(sender * Xc, Xc)], ssem.at[d], rsem.at[sender],
            device_id={"space": d}, device_id_type=MESH)

    def gather_start(src, dst, ssem, rsem):
        for d in range(C):
            @pl.when(me == d)
            def _():
                dst[pl.ds(d * Xc, Xc)] = src[d]

            @pl.when(me != d)
            def _():
                gather_copy(src, dst, d, ssem, rsem, me).start()

    def gather_wait_recv(src, dst, ssem, rsem):
        for sender in range(n):
            @pl.when(me != sender)
            def _():
                gather_copy(src, dst, 0, ssem, rsem, sender).wait_recv()

    def gather_wait_send(src, dst, ssem, rsem):
        for d in range(C):
            @pl.when(me != d)
            def _():
                gather_copy(src, dst, d, ssem, rsem, me).wait_send()

    gather_start(gs, csw, css, csr)

    fine_masks = edge_masks((Z, Y), 0, 1)

    def lap(d, i):
        v = u[d, i]
        summed = u[d, i - 1] + u[d, i + 1]
        zu, zl, yu, yl = masked_shifts(v, fine_masks, 0, 1)
        summed = summed + (zu + zl) + (yu + yl)
        return v + VISCOSITY * (summed - 6.0 * v)

    u_x.wait()

    def predict(i):
        pr[0, i] = lap(0, i + 1) + BUOYANCY * (2.0 * m[i - 1 + H] - 1.0)
        pr[1, i] = lap(1, i + 1)
        pr[2, i] = lap(2, i + 1)

    planes(1, X + 1, predict)
    pr[1, 0] = jnp.where(has_left, lap(1, 1), 0.0)
    pr[1, X + 1] = jnp.where(has_right, lap(1, X + 2), 0.0)

    def aim(i):
        zu, zl, _, _ = masked_shifts(pr[0, i], fine_masks, 0, 1)
        _, _, yu, yl = masked_shifts(pr[2, i], fine_masks, 0, 1)
        t[i - 1 + H] = -0.5 * ((zu - zl) + (pr[1, i + 1] - pr[1, i - 1]) + (yu - yl))

    planes(1, X + 1, aim)
    t_x.start()

    m_x.wait()

    def weigh(i):
        v = m[i]
        up, low = 0.5 * (v + m[i + 1]), 0.5 * (v + m[i - 1])
        wx[i] = up
        total = up + low
        for ref, mask, s in zip((wzu, wzl, wyu, wyl), fine_masks, shifts(v, 0, 1)):
            total = total + 0.5 * (v + jnp.where(mask, s, 0.0))
            ref[i] = jnp.where(mask, 0.5 * (v + s), 0.0)
        dg[i] = total
        rd[i] = jnp.where(v > 0.0, OMEGA / jnp.where(v > 0.0, total, 1.0), 0.0)

    wx[0] = 0.5 * (m[0] + m[1])
    planes(1, X + 2 * H - 1, weigh)

    mc[0:HC] = restricted(HC, lambda j: m[2 * j] + m[2 * j + 1])
    mc[HC + Xc:] = restricted(HC, lambda j: m[H + X + 2 * j] + m[H + X + 2 * j + 1])
    W = Xc + 2 * HC - 2
    mid = mc[1:1 + W]
    coarse_masks = edge_masks((W, Zc, Yc), 1, 2)
    cw[0] = 0.125 * (mid + mc[2:2 + W])
    cw[1] = 0.125 * (mid + mc[0:W])
    total = cw[0] + cw[1]
    for k, (mask, s) in enumerate(zip(coarse_masks, shifts(mid, 1, 2))):
        total = total + 0.125 * (mid + jnp.where(mask, s, 0.0))
        cw[2 + k] = jnp.where(mask, 0.125 * (mid + s), 0.0)
    cw[6] = jnp.where(mid > 0.0, OMEGA / jnp.where(mid > 0.0, total, 1.0), 0.0)

    def flux(p, i):
        v = p[i]
        zu, zl, yu, yl = shifts(v, 0, 1)
        s = wx[i] * p[i + 1] + wx[i - 1] * p[i - 1]
        s = s + (wzu[i] * zu + wzl[i] * zl)
        return v, s + (wyu[i] * yu + wyl[i] * yl)

    def smooth(src, dst, width):
        def one(i):
            v, s = flux(src, i)
            dst[i] = (1.0 - OMEGA) * v + rd[i] * (t[i] + s)

        planes(H - width, H + X + width, one)

    def residual(p, i):
        v, s = flux(p, i)
        return t[i] - dg[i] * v + s

    def coarse_correct(p, extra):
        first = H - 2 * (HC - 1)
        left = restricted(W, lambda j: residual(p, first + 2 * j) + residual(p, first + 2 * j + 1))
        v = cw[6] * left
        for _ in range(SWEEPS - 1):
            zu, zl, yu, yl = shifts(v, 1, 2)
            s = cw[0] * x_up(v) + cw[1] * x_down(v) + (cw[2] * zu + cw[3] * zl) + (cw[4] * yu + cw[5] * yl)
            v = (1.0 - OMEGA) * v + cw[6] * (left + s)
        prolonged(v[HC - 2:W - (HC - 2)])

        def add(j, carry):
            c = rs[pl.ds(pl.multiple_of(j * Z, Z), Z), :]
            for h in range(2):
                p[H - 2 + 2 * j + h] = p[H - 2 + 2 * j + h] + c
            return carry

        lax.fori_loop(0, Xc + 2, add, 0)

    t_x.wait()

    def first_guess(i):
        pa[i] = rd[i] * t[i]

    planes(1, X + 2 * H - 1, first_guess)
    coarse_correct(pa, 0)
    smooth(pa, pb, 0)
    p_x.start()

    grid_masks = edge_masks((n * Xc, Zc, Yc), 1, 2)

    def substep(v):
        a = mcw[...] * RATE
        zu, zl, yu, yl = masked_shifts(v, grid_masks, 1, 2)
        s = x_up(v) + x_down(v) + (zu + zl) + (yu + yl)
        return v + a * (s - 6.0 * v)

    def steps(ref, times):
        def one(k, carry):
            ref[...] = substep(ref[...])
            return carry

        lax.fori_loop(0, 2 * times, one, 0)

    for k in range(1, n):
        mc_copy(k, lax.rem(me + n - k, n)).wait_recv()

    @pl.when(me < C)
    def _():
        gather_wait_recv(gs, csw, css, csr)
        steps(csw, 1)

    p_x.wait()
    smooth(pb, pa, H - 1)
    coarse_correct(pa, 1)
    smooth(pa, pc, 1)

    def finish(i):
        v = pc[i]
        zu, zl, yu, yl = masked_shifts(v, fine_masks, 0, 1)
        k = i - H + 1
        half = 0.5 * m[i]
        out[0, i - H] = pr[0, k] - half * (zu - zl)
        out[1, i - H] = pr[1, k] - half * (pc[i + 1] - pc[i - 1])
        out[2, i - H] = pr[2, k] - half * (yu - yl)

    planes(H, H + X, finish)
    for d in range(C):
        ce[d] = restricted(Xc, lambda j: out[d, 2 * j] + out[d, 2 * j + 1])
    gather_start(ce, cew, ces, cer)

    def final_copy(d, peer):
        return pltpu.make_async_remote_copy(
            part.at[len(spans), pl.ds(peer * Xc, Xc)], wfin.at[d], fs.at[peer], fr.at[d],
            device_id={"space": peer}, device_id_type=MESH)

    @pl.when(me < C)
    def _():
        gather_wait_recv(ce, cew, ces, cer)
        part[0] = jnp.where(tm == 0, cew[...], cew[...] - csw[...])
        for r, s in enumerate(spans):
            def hop(target):
                return pltpu.make_async_remote_copy(
                    part.at[r], recv.at[r], ss.at[r], sr.at[r], device_id={"tm": target}, device_id_type=MESH)

            @pl.when(tm + s < ntm)
            def _():
                hop(tm + s).start()

            @pl.when(tm >= s)
            def _():
                hop(tm).wait_recv()
                steps(recv.at[r], s)
                part[r + 1] = part[r] + recv[r]

            @pl.when(tm < s)
            def _():
                part[r + 1] = part[r]

        for peer in range(n):
            @pl.when(me != peer)
            def _():
                final_copy(me, peer).start()

            @pl.when(me == peer)
            def _():
                wfin[peer if peer < C else 0] = part[len(spans), pl.ds(peer * Xc, Xc)]

    for d in range(C):
        @pl.when(me != d)
        def _():
            final_copy(d, d).wait_recv()

        prolonged(wfin[d] - ce[d])

        def add(j, carry):
            c = rs[pl.ds(pl.multiple_of(j * Z, Z), Z), :]
            for h in range(2):
                out[d, 2 * j + h] = out[d, 2 * j + h] + c
            return carry

        lax.fori_loop(0, Xc, add, 0)

    for k in range(1, n):
        mc_copy(k, me).wait_send()
    gather_wait_send(gs, csw, css, csr)
    gather_wait_send(ce, cew, ces, cer)

    @pl.when(me < C)
    def _():
        for r, s in enumerate(spans):
            @pl.when(tm + s < ntm)
            def _():
                pltpu.make_async_remote_copy(
                    part.at[r], recv.at[r], ss.at[r], sr.at[r],
                    device_id={"tm": tm + s}, device_id_type=MESH).wait_send()
        for peer in range(n):
            @pl.when(me != peer)
            def _():
                final_copy(me, peer).wait_send()


def body(n, ntm, start_states, labels):
    C, Z, X, Y = start_states.shape[1:]
    Xc, Zc, Yc = X // 2, Z // 2, Y // 2
    HC = H // 2
    spans = []
    while (1 << len(spans)) < ntm:
        spans.append(1 << len(spans))
    mobility = 1.0 / (1.0 + 3.0 * labels.astype(f32))
    u_in = jnp.swapaxes(start_states[0], 1, 2)
    m_in = jnp.swapaxes(mobility, 0, 1)
    wide = pltpu.VMEM((X + 2 * H, Z, Y), f32)
    W = Xc + 2 * HC - 2
    grid = pltpu.VMEM((n * Xc, Zc, Yc), f32)
    rows = max(W, Xc + 2) * Z
    R = len(spans)
    dma = pltpu.SemaphoreType.DMA
    scratch = [
        pltpu.VMEM((C, X + 4, Z, Y), f32), wide, pltpu.VMEM((C, X + 2, Z, Y), f32),
        wide, wide, wide, wide, wide, wide, wide, wide, wide, wide, wide,
        pltpu.VMEM((rows, Y), f32), pltpu.VMEM((rows, Yc), f32),
        pltpu.VMEM((Xc + 2 * HC, Zc, Yc), f32), pltpu.VMEM((7, W, Zc, Yc), f32),
        pltpu.VMEM((C, Xc, Zc, Yc), f32), grid, grid, grid, pltpu.VMEM((C, Xc, Zc, Yc), f32),
        pltpu.VMEM((R + 1, n * Xc, Zc, Yc), f32), pltpu.VMEM((max(R, 1), n * Xc, Zc, Yc), f32),
        pltpu.VMEM((C, Xc, Zc, Yc), f32),
        pltpu.VMEM((Y, Yc), jnp.bfloat16), pltpu.VMEM((Yc, Y), jnp.bfloat16),
        dma((2,)), dma((2, C)), dma((2, C)), dma((2, 1)), dma((2, 1)), dma((2, 1)), dma((2, 1)),
        dma((2, 1)), dma((2, 1)), dma((n,)), dma((n,)), dma((C,)), dma((n,)), dma((C,)), dma((n,)),
        dma((max(R, 1),)), dma((max(R, 1),)), dma((n,)), dma((C,)),
    ]
    result = pl.pallas_call(
        functools.partial(kernel, n, ntm, spans),
        out_shape=jax.ShapeDtypeStruct((C, X, Z, Y), f32),
        in_specs=[pl.BlockSpec(memory_space=pl.ANY)] * 2,
        out_specs=pl.BlockSpec(memory_space=pltpu.VMEM),
        scratch_shapes=scratch,
        compiler_params=pltpu.CompilerParams(
            collective_id=0, has_side_effects=True, vmem_limit_bytes=40 * 1024 * 1024),
    )(u_in, m_in)
    return jnp.swapaxes(result, 1, 2)[None]


def solution(mesh):
    in_specs = (P("tm", None, None, "space", None), P(None, "space", None))
    out_specs = P("tm", None, None, "space", None)
    fn = functools.partial(body, mesh.shape["space"], mesh.shape["tm"])
    return jax.shard_map(fn, mesh=mesh, in_specs=in_specs, out_specs=out_specs, check_vma=False)
```

time: 461 us -> 51.8 us (0.11)
  the two profiles are of different devices: /device:TPU:25 before, /device:TPU:31 now
where the time goes in v1:
time: 51.8 us; the launch traced here: 51.6 us
  Pallas kernels  47.5 us (92%)
  local copies, waits for them, and re-layouts  2.93 us (6%)
  other arithmetic  1.13 us (2%)
    pallas_call x1, Pallas kernels, body(): pl.pallas_call(functools.partial(kernel, n, ntm, spans), out_shape=jax.Sh...  47.5 us
    unnamed x1, local copies, waits for them, and re-layouts  1.59 us
    broadcast_in_dim x1, local copies, waits for them, and re-layouts, body(): return jnp.swapaxes(result, 1, 2)[None]  1.34 us
    transpose x1, other arithmetic, body(): m_in = jnp.swapaxes(mobility, 0, 1)  1.13 us

profile of v1, /device:TPU:31, one launch (start us, length us, event | category | flops | bytes accessed | tf_op | source)
XLA Modules:
  0.0 51.6 jit_solution(12665875434194521183)
XLA Ops:
  0.0 1.1 %fusion.3.m_in = f32[16,16,256]{2,1,0:T(8,128)S(1)} fusion(s32[16,16,256]{2,1,0:T(8,128)} %param.3), kind=kLoop, calls=%fused_computation.5 | loop fusion | flops 262144 | bytes 524288 | tf_op jit(solution)/shard_map/transpose | solution.py:462
  1.1 1.6 %copy.16 = f32[1,3,16,16,256]{4,2,3,1,0:T(8,128)S(1)} copy(f32[1,3,16,16,256]{4,3,2,1,0:T(8,128)} %param.2) | data formatting | bytes 1572864 | tf_op args[0]
  2.7 47.5 %shard_map.28 = f32[3,16,16,256]{3,2,1,0:T(8,128)S(1)} custom-call(f32[3,16,16,256]{3,2,1,0:T(8,128)S(1)} %bitcast.11, f32[16,16,256]{2,1,0:T(8,128)S(1)} %fusion.3.m_in), custom_call_target="tpu_custom_call" | custom-call | tf_op jit(solution)/shard_map/pallas_call | solution.py:482
  50.3 1.3 %copy.5 = f32[1,3,16,16,256]{4,3,2,1,0:T(8,128)} copy(f32[1,3,16,16,256]{4,2,3,1,0:T(8,128)S(1)} %bitcast.10) | data formatting | bytes 1572864 | tf_op jit(solution)/shard_map/broadcast_in_dim | solution.py:491

commit v2 on v1

--- a/solution.py
+++ b/solution.py
@@ -46,14 +46,22 @@
     return [jnp.where(m, s, 0.0) for m, s in zip(masks, shifts(v, zaxis, yaxis))]
 
 
-def planes(lo, hi, fn, step=2):
+def planes(lo, hi, fn, step=8):
     def some(k, carry):
         for j in range(step):
             fn(lo + k * step + j)
         return carry
 
-    assert (hi - lo) % step == 0
-    lax.fori_loop(0, (hi - lo) // step, some, 0)
+    turns = (hi - lo) // step
+    if turns > 1:
+        lax.fori_loop(0, turns, some, 0)
+        lo = lo + turns * step
+    for i in range(lo, hi):
+        fn(i)
+
+
+def rows_at(j, size):
+    return pl.ds(j * size if isinstance(j, int) else pl.multiple_of(j * size, size), size)
 
 
 def x_up(v):
@@ -64,19 +72,19 @@
     return jnp.concatenate([jnp.zeros_like(v[:1]), v[:-1]], axis=0)
 
 
-def kernel(n, ntm, spans, u_in, m_in, out, u, m, pr, t, pa, pb, pc, rd, dg, wx, wzu, wzl, wyu, wyl,
+def kernel(n, ntm, spans, u_in, l_in, out, u_raw, l_raw, u, m, pr, t, pa, pb, pc, rd, dg, wx, wzu, wzl, wyu, wyl,
            rs, rz, mc, cw, ce, mcw, csw, cew, gs, part, recv, wfin, down, dup,
            local_sem, us, ur, ms, mr, ts, tr, ps, pr_sem, mcs, mcr, css, csr, ces, cer, ss, sr, fs, fr):
     me, tm = lax.axis_index("space"), lax.axis_index("tm")
-    X, Z, Y = u_in.shape[1:]
+    Z, X, Y = u_in.shape[1:]
     Xc, Zc, Yc = X // 2, Z // 2, Y // 2
     HC = H // 2
     C = u_in.shape[0]
     has_left, has_right = me > 0, me < n - 1
 
     loads = [
-        pltpu.make_async_copy(u_in, u.at[:, pl.ds(2, X)], local_sem.at[0]),
-        pltpu.make_async_copy(m_in, m.at[pl.ds(H, X)], local_sem.at[1]),
+        pltpu.make_async_copy(u_in, u_raw, local_sem.at[0]),
+        pltpu.make_async_copy(l_in, l_raw, local_sem.at[1]),
     ]
     for c in loads:
         c.start()
@@ -115,12 +123,17 @@
     col = lax.broadcasted_iota(jnp.int32, (Yc, Y), 1)
     dup[...] = jnp.where(row == lax.div(col, 2), 1.0, 0.0).astype(jnp.bfloat16)
 
+    def fill(lo, hi, plane_sum, base=0):
+        def one(j):
+            rs[rows_at(base + j, Z), :] = plane_sum(j)
+
+        planes(lo, hi, one, 4)
+
     def restricted(count_c, plane_sum):
-        def one(j, carry):
-            rs[pl.ds(pl.multiple_of(j * Z, Z), Z), :] = plane_sum(j)
-            return carry
-
-        lax.fori_loop(0, count_c, one, 0)
+        fill(0, count_c, plane_sum)
+        return averaged(count_c)
+
+    def averaged(count_c):
         rows = count_c * Z
         rz[0:rows, :] = split_dot(rs[0:rows, :], down[...])
         half = rows // 2
@@ -176,8 +189,11 @@
     def plane_view(ref):
         return lambda first, width: ref.at[pl.ds(first, width)]
 
-    for c in loads:
-        c.wait()
+    loads[0].wait()
+    for d in range(C):
+        u[d, 2:2 + X] = jnp.swapaxes(u_raw[d], 0, 1)
+    loads[1].wait()
+    m[H:H + X] = jnp.swapaxes(1.0 - 0.75 * l_raw[...].astype(f32), 0, 1)
     pl.semaphore_wait(barrier, count)
 
     u_x = Exchange([(lambda f, w, d=d: u.at[d, pl.ds(f, w)], 2, 2 if d == 1 else 1) for d in range(C)], us, ur)
@@ -194,7 +210,8 @@
     mc[HC:HC + Xc] = mine
     mcw[pl.ds(me * Xc, Xc)] = mine
     for d in range(C):
-        gs[d] = restricted(Xc, lambda j: u[d, 2 + 2 * j] + u[d, 3 + 2 * j])
+        fill(0, Xc, lambda j: u[d, 2 + 2 * j] + u[d, 3 + 2 * j], d * Xc)
+    gs[...] = averaged(C * Xc).reshape(C, Xc, Zc, Yc)
 
     def mc_copy(k, src):
         peer = lax.rem(me + k, n)
@@ -202,9 +219,6 @@
         return pltpu.make_async_remote_copy(
             at, mcw.at[pl.ds(src * Xc, Xc)], mcs.at[k], mcr.at[k], device_id={"space": peer}, device_id_type=MESH)
 
-    for k in range(1, n):
-        mc_copy(k, me).start()
-
     def gather_copy(src, dst, d, ssem, rsem, sender):
         return pltpu.make_async_remote_copy(
             src.at[d], dst.at[pl.ds(sender * Xc, Xc)], ssem.at[d], rsem.at[sender],
@@ -231,8 +245,6 @@
             @pl.when(me != d)
             def _():
                 gather_copy(src, dst, d, ssem, rsem, me).wait_send()
-
-    gather_start(gs, csw, css, csr)
 
     fine_masks = edge_masks((Z, Y), 0, 1)
 
@@ -298,20 +310,24 @@
         s = s + (wzu[i] * zu + wzl[i] * zl)
         return v, s + (wyu[i] * yu + wyl[i] * yl)
 
-    def smooth(src, dst, width):
+    def smooth(src, dst, lo, hi):
         def one(i):
             v, s = flux(src, i)
             dst[i] = (1.0 - OMEGA) * v + rd[i] * (t[i] + s)
 
-        planes(H - width, H + X + width, one)
+        planes(lo, hi, one)
 
     def residual(p, i):
         v, s = flux(p, i)
         return t[i] - dg[i] * v + s
 
-    def coarse_correct(p, extra):
-        first = H - 2 * (HC - 1)
-        left = restricted(W, lambda j: residual(p, first + 2 * j) + residual(p, first + 2 * j + 1))
+    first = H - 2 * (HC - 1)
+
+    def leftover(p, lo, hi):
+        fill(lo, hi, lambda j: residual(p, first + 2 * j) + residual(p, first + 2 * j + 1))
+
+    def coarse_correct(p):
+        left = averaged(W)
         v = cw[6] * left
         for _ in range(SWEEPS - 1):
             zu, zl, yu, yl = shifts(v, 1, 2)
@@ -319,24 +335,29 @@
             v = (1.0 - OMEGA) * v + cw[6] * (left + s)
         prolonged(v[HC - 2:W - (HC - 2)])
 
-        def add(j, carry):
-            c = rs[pl.ds(pl.multiple_of(j * Z, Z), Z), :]
+        def add(j):
+            c = rs[rows_at(j, Z), :]
             for h in range(2):
                 p[H - 2 + 2 * j + h] = p[H - 2 + 2 * j + h] + c
-            return carry
-
-        lax.fori_loop(0, Xc + 2, add, 0)
+
+        planes(0, Xc + 2, add, 5)
 
     t_x.wait()
+    for k in range(1, n):
+        mc_copy(k, me).start()
+    gather_start(gs, csw, css, csr)
 
     def first_guess(i):
         pa[i] = rd[i] * t[i]
 
     planes(1, X + 2 * H - 1, first_guess)
-    coarse_correct(pa, 0)
-    smooth(pa, pb, 0)
+    leftover(pa, 0, W)
+    coarse_correct(pa)
+    smooth(pa, pb, H, H + X)
     p_x.start()
 
+    smooth(pb, pa, H + 1, H + X - 1)
+    leftover(pa, HC, HC + Xc - 2)
     grid_masks = edge_masks((n * Xc, Zc, Yc), 1, 2)
 
     def substep(v):
@@ -361,9 +382,12 @@
         steps(csw, 1)
 
     p_x.wait()
-    smooth(pb, pa, H - 1)
-    coarse_correct(pa, 1)
-    smooth(pa, pc, 1)
+    smooth(pb, pa, 1, H + 1)
+    smooth(pb, pa, H + X - 1, X + 2 * H - 1)
+    leftover(pa, 0, HC)
+    leftover(pa, HC + Xc - 2, W)
+    coarse_correct(pa)
+    smooth(pa, pc, H - 1, H + X + 1)
 
     def finish(i):
         v = pc[i]
@@ -376,7 +400,8 @@
 
     planes(H, H + X, finish)
     for d in range(C):
-        ce[d] = restricted(Xc, lambda j: out[d, 2 * j] + out[d, 2 * j + 1])
+        fill(0, Xc, lambda j: out[d, 2 * j] + out[d, 2 * j + 1], d * Xc)
+    ce[...] = averaged(C * Xc).reshape(C, Xc, Zc, Yc)
     gather_start(ce, cew, ces, cer)
 
     def final_copy(d, peer):
@@ -421,15 +446,14 @@
         def _():
             final_copy(d, d).wait_recv()
 
-        prolonged(wfin[d] - ce[d])
-
-        def add(j, carry):
-            c = rs[pl.ds(pl.multiple_of(j * Z, Z), Z), :]
+    prolonged((wfin[...] - ce[...]).reshape(C * Xc, Zc, Yc))
+    for d in range(C):
+        def add(j):
+            c = rs[rows_at(d * Xc + j, Z), :]
             for h in range(2):
                 out[d, 2 * j + h] = out[d, 2 * j + h] + c
-            return carry
-
-        lax.fori_loop(0, Xc, add, 0)
+
+        planes(0, Xc, add, 4)
 
     for k in range(1, n):
         mc_copy(k, me).wait_send()
@@ -457,16 +481,14 @@
     spans = []
     while (1 << len(spans)) < ntm:
         spans.append(1 << len(spans))
-    mobility = 1.0 / (1.0 + 3.0 * labels.astype(f32))
-    u_in = jnp.swapaxes(start_states[0], 1, 2)
-    m_in = jnp.swapaxes(mobility, 0, 1)
     wide = pltpu.VMEM((X + 2 * H, Z, Y), f32)
     W = Xc + 2 * HC - 2
     grid = pltpu.VMEM((n * Xc, Zc, Yc), f32)
-    rows = max(W, Xc + 2) * Z
+    rows = max(W, Xc + 2, C * Xc) * Z
     R = len(spans)
     dma = pltpu.SemaphoreType.DMA
     scratch = [
+        pltpu.VMEM((C, Z, X, Y), f32), pltpu.VMEM((Z, X, Y), jnp.int32),
         pltpu.VMEM((C, X + 4, Z, Y), f32), wide, pltpu.VMEM((C, X + 2, Z, Y), f32),
         wide, wide, wide, wide, wide, wide, wide, wide, wide, wide, wide,
         pltpu.VMEM((rows, Y), f32), pltpu.VMEM((rows, Yc), f32),
@@ -487,7 +509,7 @@
         scratch_shapes=scratch,
         compiler_params=pltpu.CompilerParams(
             collective_id=0, has_side_effects=True, vmem_limit_bytes=40 * 1024 * 1024),
-    )(u_in, m_in)
+    )(start_states[0], labels)
     return jnp.swapaxes(result, 1, 2)[None]
 
 

time: 51.8 us -> 44.4 us (0.86)
  Pallas kernels: 47.5 us -> 40.8 us
  other arithmetic: 1.13 us -> 0 us
    pallas_call x1, Pallas kernels: 47.5 us -> 40.8 us  [body(): pl.pallas_call(functools.partial(kernel, n, ntm, spans), out_shape=jax.Sh...]
    transpose x1 -> x0, other arithmetic: 1.13 us -> none  [body(): m_in = jnp.swapaxes(mobility, 0, 1)]
    unnamed x1 -> x4, local copies, waits for them, and re-layouts: 1.59 us -> 2.08 us
where the time goes in v2:
time: 44.4 us; the launch traced here: 44.3 us
  Pallas kernels  40.8 us (92%)
  local copies, waits for them, and re-layouts  3.42 us (8%)
    pallas_call x1, Pallas kernels, body(): pl.pallas_call(functools.partial(kernel, n, ntm, spans), out_shape=jax.Sh...  40.8 us
    unnamed x4, local copies, waits for them, and re-layouts  2.08 us
    broadcast_in_dim x1, local copies, waits for them, and re-layouts, body(): return jnp.swapaxes(result, 1, 2)[None]  1.34 us

profile of v2, /device:TPU:31, one launch (start us, length us, event | category | flops | bytes accessed | tf_op | source)
XLA Modules:
  0.0 44.3 jit_solution(16897785473635195653)
XLA Ops:
  0.0 0.0 copy-start
  0.0 1.1 %copy-done = f32[1,3,16,16,256]{4,3,2,1,0:T(8,128)S(1)} copy-done((f32[1,3,16,16,256]{4,3,2,1,0:T(8,128)S(1)}, f32[1,3,16,16,256]{4,3,2,1,0:T(8,128)}, u32[]{:S(2)}) %copy-start) | copy-done | bytes 786456
  1.1 0.0 copy-start.1
  1.1 0.9 %copy-done.1 = s32[16,16,256]{2,1,0:T(8,128)S(1)} copy-done((s32[16,16,256]{2,1,0:T(8,128)S(1)}, s32[16,16,256]{2,1,0:T(8,128)}, u32[]{:S(2)}) %copy-start.1) | copy-done | bytes 262168
  2.1 40.8 %shard_map.28 = f32[3,16,16,256]{3,2,1,0:T(8,128)S(1)} custom-call(f32[3,16,16,256]{3,2,1,0:T(8,128)S(1)} %bitcast.5, s32[16,16,256]{2,1,0:T(8,128)S(1)} %copy-done.1), custom_call_target="tpu_custom_call" | custom-call | tf_op jit(solution)/shard_map/pallas_call | solution.py:504
  42.9 1.3 %copy.3 = f32[1,3,16,16,256]{4,3,2,1,0:T(8,128)} copy(f32[1,3,16,16,256]{4,2,3,1,0:T(8,128)S(1)} %bitcast.4) | data formatting | bytes 1572864 | tf_op jit(solution)/shard_map/broadcast_in_dim | solution.py:513
Async XLA Ops:
  0.0 1.1 %copy-start = (f32[1,3,16,16,256]{4,3,2,1,0:T(8,128)S(1)}, f32[1,3,16,16,256]{4,3,2,1,0:T(8,128)}, u32[]{:S(2)}) copy-start(f32[1,3,16,16,256]{4,3,2,1,0:T(8,128)} %param.2) | copy-start | bytes 2359300
  1.1 0.9 %copy-start.1 = (s32[16,16,256]{2,1,0:T(8,128)S(1)}, s32[16,16,256]{2,1,0:T(8,128)}, u32[]{:S(2)}) copy-start(s32[16,16,256]{2,1,0:T(8,128)} %l_in.1) | copy-start | bytes 786436

commit v3 on v2

--- a/solution.py
+++ b/solution.py
@@ -73,13 +73,15 @@
 
 
 def kernel(n, ntm, spans, u_in, l_in, out, u_raw, l_raw, u, m, pr, t, pa, pb, pc, rd, dg, wx, wzu, wzl, wyu, wyl,
-           rs, rz, mc, cw, ce, mcw, csw, cew, gs, part, recv, wfin, down, dup,
-           local_sem, us, ur, ms, mr, ts, tr, ps, pr_sem, mcs, mcr, css, csr, ces, cer, ss, sr, fs, fr):
+           rs, rz, mc, cw, ce, mcw, csw, part, vb, down, dup,
+           local_sem, us, ur, ms, mr, ts, tr, ps, pr_sem, mcs, mcr, css, csr, ss, sr, fs, fr):
     me, tm = lax.axis_index("space"), lax.axis_index("tm")
     Z, X, Y = u_in.shape[1:]
     Xc, Zc, Yc = X // 2, Z // 2, Y // 2
     HC = H // 2
     C = u_in.shape[0]
+    hm = (vb.shape[2] - Xc) // 2
+    R = len(spans)
     has_left, has_right = me > 0, me < n - 1
 
     loads = [
@@ -90,9 +92,16 @@
         c.start()
 
     barrier = pltpu.get_barrier_semaphore()
-    for k in range(1, n):
-        pl.semaphore_signal(barrier, inc=1, device_id={"space": lax.rem(me + k, n)}, device_id_type=MESH)
-    count = n - 1
+    count = jnp.where(has_left, 1, 0) + jnp.where(has_right, 1, 0)
+
+    @pl.when(has_left)
+    def _():
+        pl.semaphore_signal(barrier, inc=1, device_id={"space": me - 1}, device_id_type=MESH)
+
+    @pl.when(has_right)
+    def _():
+        pl.semaphore_signal(barrier, inc=1, device_id={"space": me + 1}, device_id_type=MESH)
+
     for s in spans:
         @pl.when(tm >= s)
         def _():
@@ -109,12 +118,18 @@
         u[:, 0:2] = jnp.zeros((C, 2, Z, Y), f32)
         for ref in (m, t, pb):
             ref[0:H] = jnp.zeros((H, Z, Y), f32)
+        mcw[0:hm] = jnp.zeros((hm, Zc, Yc), f32)
+        csw[:, 0:2] = jnp.zeros((C, 2, Zc, Yc), f32)
+        vb[:, :, 0:hm] = jnp.zeros(vb.shape[:2] + (hm, Zc, Yc), f32)
 
     @pl.when(jnp.logical_not(has_right))
     def _():
         u[:, X + 2:X + 4] = jnp.zeros((C, 2, Z, Y), f32)
         for ref in (m, t, pb):
             ref[X + H:X + 2 * H] = jnp.zeros((H, Z, Y), f32)
+        mcw[hm + Xc:] = jnp.zeros((hm, Zc, Yc), f32)
+        csw[:, 2 + Xc:] = jnp.zeros((C, 2, Zc, Yc), f32)
+        vb[:, :, hm + Xc:] = jnp.zeros(vb.shape[:2] + (hm, Zc, Yc), f32)
 
     row = lax.broadcasted_iota(jnp.int32, (Y, Yc), 0)
     col = lax.broadcasted_iota(jnp.int32, (Y, Yc), 1)
@@ -153,7 +168,7 @@
         return pltpu.make_async_remote_copy(src, dst, ssem, rsem, device_id={"space": me + 1}, device_id_type=MESH)
 
     class Exchange:
-        def __init__(self, items, ssem, rsem):
+        def __init__(self, items, ssem, rsem, X=X):
             self.left, self.right = [], []
             for k, (at, first, width) in enumerate(items):
                 self.left.append(to_left(at(first, width), at(first + X, width), ssem.at[0, k], rsem.at[0, k]))
@@ -203,48 +218,14 @@
     u_x.start()
     m_x.start()
 
-    def own_rows(ref):
-        return ref.at[pl.ds(me * Xc, Xc)]
-
     mine = restricted(Xc, lambda j: m[H + 2 * j] + m[H + 2 * j + 1])
     mc[HC:HC + Xc] = mine
-    mcw[pl.ds(me * Xc, Xc)] = mine
+    mcw[hm:hm + Xc] = mine
     for d in range(C):
         fill(0, Xc, lambda j: u[d, 2 + 2 * j] + u[d, 3 + 2 * j], d * Xc)
-    gs[...] = averaged(C * Xc).reshape(C, Xc, Zc, Yc)
-
-    def mc_copy(k, src):
-        peer = lax.rem(me + k, n)
-        at = mc.at[pl.ds(HC, Xc)]
-        return pltpu.make_async_remote_copy(
-            at, mcw.at[pl.ds(src * Xc, Xc)], mcs.at[k], mcr.at[k], device_id={"space": peer}, device_id_type=MESH)
-
-    def gather_copy(src, dst, d, ssem, rsem, sender):
-        return pltpu.make_async_remote_copy(
-            src.at[d], dst.at[pl.ds(sender * Xc, Xc)], ssem.at[d], rsem.at[sender],
-            device_id={"space": d}, device_id_type=MESH)
-
-    def gather_start(src, dst, ssem, rsem):
-        for d in range(C):
-            @pl.when(me == d)
-            def _():
-                dst[pl.ds(d * Xc, Xc)] = src[d]
-
-            @pl.when(me != d)
-            def _():
-                gather_copy(src, dst, d, ssem, rsem, me).start()
-
-    def gather_wait_recv(src, dst, ssem, rsem):
-        for sender in range(n):
-            @pl.when(me != sender)
-            def _():
-                gather_copy(src, dst, 0, ssem, rsem, sender).wait_recv()
-
-    def gather_wait_send(src, dst, ssem, rsem):
-        for d in range(C):
-            @pl.when(me != d)
-            def _():
-                gather_copy(src, dst, d, ssem, rsem, me).wait_send()
+    csw[:, 2:2 + Xc] = averaged(C * Xc).reshape(C, Xc, Zc, Yc)
+    mc_x = Exchange([(plane_view(mcw), hm, hm)], mcs, mcr, Xc)
+    cs_x = Exchange([(lambda f, w: csw.at[:, pl.ds(f, w)], 2, 2)], css, csr, Xc)
 
     fine_masks = edge_masks((Z, Y), 0, 1)
 
@@ -343,9 +324,8 @@
         planes(0, Xc + 2, add, 5)
 
     t_x.wait()
-    for k in range(1, n):
-        mc_copy(k, me).start()
-    gather_start(gs, csw, css, csr)
+    mc_x.start()
+    cs_x.start()
 
     def first_guess(i):
         pa[i] = rd[i] * t[i]
@@ -358,29 +338,20 @@
 
     smooth(pb, pa, H + 1, H + X - 1)
     leftover(pa, HC, HC + Xc - 2)
-    grid_masks = edge_masks((n * Xc, Zc, Yc), 1, 2)
-
-    def substep(v):
-        a = mcw[...] * RATE
-        zu, zl, yu, yl = masked_shifts(v, grid_masks, 1, 2)
-        s = x_up(v) + x_down(v) + (zu + zl) + (yu + yl)
-        return v + a * (s - 6.0 * v)
-
-    def steps(ref, times):
-        def one(k, carry):
-            ref[...] = substep(ref[...])
-            return carry
-
-        lax.fori_loop(0, 2 * times, one, 0)
-
-    for k in range(1, n):
-        mc_copy(k, lax.rem(me + n - k, n)).wait_recv()
-
-    @pl.when(me < C)
-    def _():
-        gather_wait_recv(gs, csw, css, csr)
-        steps(csw, 1)
-
+    def coarse_steps(v, times):
+        for _ in range(2 * times):
+            length = v.shape[0] - 2
+            off = (Xc + 2 * hm - length) // 2
+            mid = v[1:-1]
+            zu, zl, yu, yl = masked_shifts(mid, edge_masks(mid.shape, 1, 2), 1, 2)
+            s = v[2:] + v[:-2] + (zu + zl) + (yu + yl)
+            v = mid + (RATE * mcw[off:off + length]) * (s - 6.0 * mid)
+        return v
+
+    mc_x.wait()
+    cs_x.wait()
+    for d in range(C):
+        part[0, d] = jnp.where(tm == 0, 0.0, coarse_steps(csw[d], 1))
     p_x.wait()
     smooth(pb, pa, 1, H + 1)
     smooth(pb, pa, H + X - 1, X + 2 * H - 1)
@@ -402,51 +373,59 @@
     for d in range(C):
         fill(0, Xc, lambda j: out[d, 2 * j] + out[d, 2 * j + 1], d * Xc)
     ce[...] = averaged(C * Xc).reshape(C, Xc, Zc, Yc)
-    gather_start(ce, cew, ces, cer)
-
-    def final_copy(d, peer):
+
+    stages, starts = [], []
+    for s in spans:
+        starts.append(sum(stages))
+        stages.append(max(1, -(-2 * s // Xc)))
+
+    def hop(r, d, target):
         return pltpu.make_async_remote_copy(
-            part.at[len(spans), pl.ds(peer * Xc, Xc)], wfin.at[d], fs.at[peer], fr.at[d],
-            device_id={"space": peer}, device_id_type=MESH)
-
-    @pl.when(me < C)
-    def _():
-        gather_wait_recv(ce, cew, ces, cer)
-        part[0] = jnp.where(tm == 0, cew[...], cew[...] - csw[...])
-        for r, s in enumerate(spans):
-            def hop(target):
-                return pltpu.make_async_remote_copy(
-                    part.at[r], recv.at[r], ss.at[r], sr.at[r], device_id={"tm": target}, device_id_type=MESH)
-
-            @pl.when(tm + s < ntm)
+            part.at[r, d], vb.at[starts[r], d, pl.ds(hm, Xc)], ss.at[r, d], sr.at[r, d],
+            device_id={"tm": target}, device_id_type=MESH)
+
+    def send(r, d):
+        if r < R:
+            @pl.when(tm + spans[r] < ntm)
             def _():
-                hop(tm + s).start()
-
-            @pl.when(tm >= s)
-            def _():
-                hop(tm).wait_recv()
-                steps(recv.at[r], s)
-                part[r + 1] = part[r] + recv[r]
-
-            @pl.when(tm < s)
-            def _():
-                part[r + 1] = part[r]
-
-        for peer in range(n):
-            @pl.when(me != peer)
-            def _():
-                final_copy(me, peer).start()
-
-            @pl.when(me == peer)
-            def _():
-                wfin[peer if peer < C else 0] = part[len(spans), pl.ds(peer * Xc, Xc)]
-
-    for d in range(C):
-        @pl.when(me != d)
+                hop(r, d, tm + spans[r]).start()
+
+    def sides(r, q, d):
+        k = starts[r] + q
+        return Exchange([(lambda f, w: vb.at[k, d, pl.ds(f, w)], hm, 2 * spans[r] // stages[r])],
+                        fs.at[k, d], fr.at[k, d], Xc)
+
+    def advance(r, d):
+        times = spans[r] // stages[r]
+        for q in range(stages[r]):
+            sides(r, q, d).wait()
+            v = coarse_steps(vb[starts[r] + q, d, hm - 2 * times:hm + Xc + 2 * times], times)
+            if q + 1 < stages[r]:
+                vb[starts[r] + q + 1, d, hm:hm + Xc] = v
+                sides(r, q + 1, d).start()
+        part[r + 1, d] = part[r, d] + v
+        send(r + 1, d)
+
+    for d in range(C):
+        part[0, d] = ce[d] - part[0, d]
+        send(0, d)
+    for r, s in enumerate(spans):
+        @pl.when(tm < s)
         def _():
-            final_copy(d, d).wait_recv()
-
-    prolonged((wfin[...] - ce[...]).reshape(C * Xc, Zc, Yc))
+            for d in range(C):
+                part[r + 1, d] = part[r, d]
+                send(r + 1, d)
+
+        @pl.when(tm >= s)
+        def _():
+            for d in range(C):
+                hop(r, d, tm).wait_recv()
+                sides(r, 0, d).start()
+                if d > 0:
+                    advance(r, d - 1)
+            advance(r, C - 1)
+
+    prolonged((part[R] - ce[...]).reshape(C * Xc, Zc, Yc))
     for d in range(C):
         def add(j):
             c = rs[rows_at(d * Xc + j, Z), :]
@@ -455,23 +434,11 @@
 
         planes(0, Xc, add, 4)
 
-    for k in range(1, n):
-        mc_copy(k, me).wait_send()
-    gather_wait_send(gs, csw, css, csr)
-    gather_wait_send(ce, cew, ces, cer)
-
-    @pl.when(me < C)
-    def _():
-        for r, s in enumerate(spans):
-            @pl.when(tm + s < ntm)
-            def _():
-                pltpu.make_async_remote_copy(
-                    part.at[r], recv.at[r], ss.at[r], sr.at[r],
-                    device_id={"tm": tm + s}, device_id_type=MESH).wait_send()
-        for peer in range(n):
-            @pl.when(me != peer)
-            def _():
-                final_copy(me, peer).wait_send()
+    for r, s in enumerate(spans):
+        @pl.when(tm + s < ntm)
+        def _():
+            for d in range(C):
+                hop(r, d, tm + s).wait_send()
 
 
 def body(n, ntm, start_states, labels):
@@ -483,7 +450,8 @@
         spans.append(1 << len(spans))
     wide = pltpu.VMEM((X + 2 * H, Z, Y), f32)
     W = Xc + 2 * HC - 2
-    grid = pltpu.VMEM((n * Xc, Zc, Yc), f32)
+    hm = min(2 * max(spans + [1]), Xc)
+    total = sum(max(1, -(-2 * s // Xc)) for s in spans) or 1
     rows = max(W, Xc + 2, C * Xc) * Z
     R = len(spans)
     dma = pltpu.SemaphoreType.DMA
@@ -493,22 +461,22 @@
         wide, wide, wide, wide, wide, wide, wide, wide, wide, wide, wide,
         pltpu.VMEM((rows, Y), f32), pltpu.VMEM((rows, Yc), f32),
         pltpu.VMEM((Xc + 2 * HC, Zc, Yc), f32), pltpu.VMEM((7, W, Zc, Yc), f32),
-        pltpu.VMEM((C, Xc, Zc, Yc), f32), grid, grid, grid, pltpu.VMEM((C, Xc, Zc, Yc), f32),
-        pltpu.VMEM((R + 1, n * Xc, Zc, Yc), f32), pltpu.VMEM((max(R, 1), n * Xc, Zc, Yc), f32),
-        pltpu.VMEM((C, Xc, Zc, Yc), f32),
+        pltpu.VMEM((C, Xc, Zc, Yc), f32), pltpu.VMEM((Xc + 2 * hm, Zc, Yc), f32),
+        pltpu.VMEM((C, Xc + 4, Zc, Yc), f32), pltpu.VMEM((R + 1, C, Xc, Zc, Yc), f32),
+        pltpu.VMEM((total, C, Xc + 2 * hm, Zc, Yc), f32),
         pltpu.VMEM((Y, Yc), jnp.bfloat16), pltpu.VMEM((Yc, Y), jnp.bfloat16),
         dma((2,)), dma((2, C)), dma((2, C)), dma((2, 1)), dma((2, 1)), dma((2, 1)), dma((2, 1)),
-        dma((2, 1)), dma((2, 1)), dma((n,)), dma((n,)), dma((C,)), dma((n,)), dma((C,)), dma((n,)),
-        dma((max(R, 1),)), dma((max(R, 1),)), dma((n,)), dma((C,)),
+        dma((2, 1)), dma((2, 1)), dma((2, 1)), dma((2, 1)), dma((2, 1)), dma((2, 1)),
+        dma((max(R, 1), C)), dma((max(R, 1), C)), dma((total, C, 2, 1)), dma((total, C, 2, 1)),
     ]
     result = pl.pallas_call(
         functools.partial(kernel, n, ntm, spans),
         out_shape=jax.ShapeDtypeStruct((C, X, Z, Y), f32),
-        in_specs=[pl.BlockSpec(memory_space=pl.ANY)] * 2,
+        in_specs=[pl.BlockSpec(memory_space=pltpu.HBM)] * 2,
         out_specs=pl.BlockSpec(memory_space=pltpu.VMEM),
         scratch_shapes=scratch,
         compiler_params=pltpu.CompilerParams(
-            collective_id=0, has_side_effects=True, vmem_limit_bytes=40 * 1024 * 1024),
+            collective_id=0, has_side_effects=True, vmem_limit_bytes=60 * 1024 * 1024),
     )(start_states[0], labels)
     return jnp.swapaxes(result, 1, 2)[None]
 

time: 44.4 us -> 42.5 us (0.957)
  the two profiles are of different devices: /device:TPU:31 before, /device:TPU:25 now
where the time goes in v3:
time: 42.5 us; the launch traced here: 42 us
  Pallas kernels  39.6 us (93%)
  local copies, waits for them, and re-layouts  2.47 us (6%)
    pallas_call x1, Pallas kernels, body(): pl.pallas_call(functools.partial(kernel, n, ntm, spans), out_shape=jax.Sh...  39.6 us
    broadcast_in_dim x1, local copies, waits for them, and re-layouts, body(): return jnp.swapaxes(result, 1, 2)[None]  2.47 us

profile of v3, /device:TPU:25, one launch (start us, length us, event | category | flops | bytes accessed | tf_op | source)
XLA Modules:
  0.0 42.0 jit_solution(4068038224814007936)
XLA Ops:
  0.0 39.6 %shard_map.28 = f32[3,16,16,256]{3,2,1,0:T(8,128)} custom-call(f32[3,16,16,256]{3,2,1,0:T(8,128)} %bitcast.5, s32[16,16,256]{2,1,0:T(8,128)} %l_in.1), custom_call_target="tpu_custom_call" | custom-call | tf_op jit(solution)/shard_map/pallas_call | solution.py:472
  39.6 2.5 %copy.3 = f32[1,3,16,16,256]{4,3,2,1,0:T(8,128)} copy(f32[1,3,16,16,256]{4,2,3,1,0:T(8,128)} %bitcast.4) | data formatting | bytes 1572864 | tf_op jit(solution)/shard_map/broadcast_in_dim | solution.py:481

commit v4 on v3

--- a/solution.py
+++ b/solution.py
@@ -12,7 +12,8 @@
 RATE = 0.15
 CYCLES = 2
 SWEEPS = 4
-H = 10
+H = 3
+HL = SWEEPS
 MESH = pl.DeviceIdType.MESH
 f32 = jnp.float32
 
@@ -73,12 +74,11 @@
 
 
 def kernel(n, ntm, spans, u_in, l_in, out, u_raw, l_raw, u, m, pr, t, pa, pb, pc, rd, dg, wx, wzu, wzl, wyu, wyl,
-           rs, rz, mc, cw, ce, mcw, csw, part, vb, down, dup,
-           local_sem, us, ur, ms, mr, ts, tr, ps, pr_sem, mcs, mcr, css, csr, ss, sr, fs, fr):
+           rs, rz, fin, lw, cw, ce, mcw, csw, part, vb, down, dup,
+           local_sem, us, ur, ms, mr, ts, tr, ps, pr_sem, mcs, mcr, css, csr, ls, lr, ss, sr, fs, fr):
     me, tm = lax.axis_index("space"), lax.axis_index("tm")
     Z, X, Y = u_in.shape[1:]
     Xc, Zc, Yc = X // 2, Z // 2, Y // 2
-    HC = H // 2
     C = u_in.shape[0]
     hm = (vb.shape[2] - Xc) // 2
     R = len(spans)
@@ -118,6 +118,7 @@
         u[:, 0:2] = jnp.zeros((C, 2, Z, Y), f32)
         for ref in (m, t, pb):
             ref[0:H] = jnp.zeros((H, Z, Y), f32)
+        lw[:, 0:HL] = jnp.zeros((CYCLES, HL, Zc, Yc), f32)
         mcw[0:hm] = jnp.zeros((hm, Zc, Yc), f32)
         csw[:, 0:2] = jnp.zeros((C, 2, Zc, Yc), f32)
         vb[:, :, 0:hm] = jnp.zeros(vb.shape[:2] + (hm, Zc, Yc), f32)
@@ -127,6 +128,7 @@
         u[:, X + 2:X + 4] = jnp.zeros((C, 2, Z, Y), f32)
         for ref in (m, t, pb):
             ref[X + H:X + 2 * H] = jnp.zeros((H, Z, Y), f32)
+        lw[:, HL + Xc:] = jnp.zeros((CYCLES, HL, Zc, Yc), f32)
         mcw[hm + Xc:] = jnp.zeros((hm, Zc, Yc), f32)
         csw[:, 2 + Xc:] = jnp.zeros((C, 2, Zc, Yc), f32)
         vb[:, :, hm + Xc:] = jnp.zeros(vb.shape[:2] + (hm, Zc, Yc), f32)
@@ -214,18 +216,19 @@
     u_x = Exchange([(lambda f, w, d=d: u.at[d, pl.ds(f, w)], 2, 2 if d == 1 else 1) for d in range(C)], us, ur)
     m_x = Exchange([(plane_view(m), H, H)], ms, mr)
     t_x = Exchange([(plane_view(t), H, H - 1)], ts, tr)
+    l_x = [Exchange([(lambda f, w, k=k: lw.at[k, pl.ds(f, w)], HL, HL)], ls.at[k], lr.at[k], Xc) for k in range(CYCLES)]
     p_x = Exchange([(plane_view(pb), H, H)], ps, pr_sem)
     u_x.start()
     m_x.start()
 
     mine = restricted(Xc, lambda j: m[H + 2 * j] + m[H + 2 * j + 1])
-    mc[HC:HC + Xc] = mine
     mcw[hm:hm + Xc] = mine
     for d in range(C):
         fill(0, Xc, lambda j: u[d, 2 + 2 * j] + u[d, 3 + 2 * j], d * Xc)
     csw[:, 2:2 + Xc] = averaged(C * Xc).reshape(C, Xc, Zc, Yc)
     mc_x = Exchange([(plane_view(mcw), hm, hm)], mcs, mcr, Xc)
     cs_x = Exchange([(lambda f, w: csw.at[:, pl.ds(f, w)], 2, 2)], css, csr, Xc)
+    mc_x.start()
 
     fine_masks = edge_masks((Z, Y), 0, 1)
 
@@ -254,6 +257,7 @@
 
     planes(1, X + 1, aim)
     t_x.start()
+    cs_x.start()
 
     m_x.wait()
 
@@ -271,13 +275,13 @@
     wx[0] = 0.5 * (m[0] + m[1])
     planes(1, X + 2 * H - 1, weigh)
 
-    mc[0:HC] = restricted(HC, lambda j: m[2 * j] + m[2 * j + 1])
-    mc[HC + Xc:] = restricted(HC, lambda j: m[H + X + 2 * j] + m[H + X + 2 * j + 1])
-    W = Xc + 2 * HC - 2
-    mid = mc[1:1 + W]
+    W = Xc + 2 * HL
+    mc_x.wait()
+    at = hm - HL
+    mid = mcw[at:at + W]
     coarse_masks = edge_masks((W, Zc, Yc), 1, 2)
-    cw[0] = 0.125 * (mid + mc[2:2 + W])
-    cw[1] = 0.125 * (mid + mc[0:W])
+    cw[0] = 0.125 * (mid + mcw[at + 1:at + 1 + W])
+    cw[1] = 0.125 * (mid + mcw[at - 1:at - 1 + W])
     total = cw[0] + cw[1]
     for k, (mask, s) in enumerate(zip(coarse_masks, shifts(mid, 1, 2))):
         total = total + 0.125 * (mid + jnp.where(mask, s, 0.0))
@@ -302,19 +306,21 @@
         v, s = flux(p, i)
         return t[i] - dg[i] * v + s
 
-    first = H - 2 * (HC - 1)
-
     def leftover(p, lo, hi):
-        fill(lo, hi, lambda j: residual(p, first + 2 * j) + residual(p, first + 2 * j + 1))
-
-    def coarse_correct(p):
-        left = averaged(W)
+        fill(lo, hi, lambda j: residual(p, H + 2 * j) + residual(p, H + 2 * j + 1))
+
+    def coarse_correct(p, cycle, meanwhile):
+        lw[cycle, HL:HL + Xc] = averaged(Xc)
+        l_x[cycle].start()
+        meanwhile()
+        l_x[cycle].wait()
+        left = lw[cycle]
         v = cw[6] * left
         for _ in range(SWEEPS - 1):
             zu, zl, yu, yl = shifts(v, 1, 2)
             s = cw[0] * x_up(v) + cw[1] * x_down(v) + (cw[2] * zu + cw[3] * zl) + (cw[4] * yu + cw[5] * yl)
             v = (1.0 - OMEGA) * v + cw[6] * (left + s)
-        prolonged(v[HC - 2:W - (HC - 2)])
+        prolonged(v[HL - 1:W - (HL - 1)])
 
         def add(j):
             c = rs[rows_at(j, Z), :]
@@ -324,20 +330,13 @@
         planes(0, Xc + 2, add, 5)
 
     t_x.wait()
-    mc_x.start()
-    cs_x.start()
 
     def first_guess(i):
         pa[i] = rd[i] * t[i]
 
     planes(1, X + 2 * H - 1, first_guess)
-    leftover(pa, 0, W)
-    coarse_correct(pa)
-    smooth(pa, pb, H, H + X)
-    p_x.start()
-
-    smooth(pb, pa, H + 1, H + X - 1)
-    leftover(pa, HC, HC + Xc - 2)
+    leftover(pa, 0, Xc)
+
     def coarse_steps(v, times):
         for _ in range(2 * times):
             length = v.shape[0] - 2
@@ -348,16 +347,24 @@
             v = mid + (RATE * mcw[off:off + length]) * (s - 6.0 * mid)
         return v
 
-    mc_x.wait()
-    cs_x.wait()
-    for d in range(C):
-        part[0, d] = jnp.where(tm == 0, 0.0, coarse_steps(csw[d], 1))
+    def step_starts():
+        cs_x.wait()
+        for d in range(C):
+            part[0, d] = jnp.where(tm == 0, 0.0, coarse_steps(csw[d], 1))
+
+    coarse_correct(pa, 0, step_starts)
+    smooth(pa, pb, H, H + X)
+    p_x.start()
+
+    smooth(pb, pa, H + 1, H + X - 1)
+    leftover(pa, 1, Xc - 1)
+
     p_x.wait()
     smooth(pb, pa, 1, H + 1)
     smooth(pb, pa, H + X - 1, X + 2 * H - 1)
-    leftover(pa, 0, HC)
-    leftover(pa, HC + Xc - 2, W)
-    coarse_correct(pa)
+    leftover(pa, 0, 1)
+    leftover(pa, Xc - 1, Xc)
+    coarse_correct(pa, 1, lambda: None)
     smooth(pa, pc, H - 1, H + X + 1)
 
     def finish(i):
@@ -365,13 +372,13 @@
         zu, zl, yu, yl = masked_shifts(v, fine_masks, 0, 1)
         k = i - H + 1
         half = 0.5 * m[i]
-        out[0, i - H] = pr[0, k] - half * (zu - zl)
-        out[1, i - H] = pr[1, k] - half * (pc[i + 1] - pc[i - 1])
-        out[2, i - H] = pr[2, k] - half * (yu - yl)
+        fin[0, i - H] = pr[0, k] - half * (zu - zl)
+        fin[1, i - H] = pr[1, k] - half * (pc[i + 1] - pc[i - 1])
+        fin[2, i - H] = pr[2, k] - half * (yu - yl)
 
     planes(H, H + X, finish)
     for d in range(C):
-        fill(0, Xc, lambda j: out[d, 2 * j] + out[d, 2 * j + 1], d * Xc)
+        fill(0, Xc, lambda j: fin[d, 2 * j] + fin[d, 2 * j + 1], d * Xc)
     ce[...] = averaged(C * Xc).reshape(C, Xc, Zc, Yc)
 
     stages, starts = [], []
@@ -430,9 +437,10 @@
         def add(j):
             c = rs[rows_at(d * Xc + j, Z), :]
             for h in range(2):
-                out[d, 2 * j + h] = out[d, 2 * j + h] + c
+                fin[d, 2 * j + h] = fin[d, 2 * j + h] + c
 
         planes(0, Xc, add, 4)
+        out[d] = jnp.swapaxes(fin[d], 0, 1)
 
     for r, s in enumerate(spans):
         @pl.when(tm + s < ntm)
@@ -444,15 +452,14 @@
 def body(n, ntm, start_states, labels):
     C, Z, X, Y = start_states.shape[1:]
     Xc, Zc, Yc = X // 2, Z // 2, Y // 2
-    HC = H // 2
     spans = []
     while (1 << len(spans)) < ntm:
         spans.append(1 << len(spans))
     wide = pltpu.VMEM((X + 2 * H, Z, Y), f32)
-    W = Xc + 2 * HC - 2
-    hm = min(2 * max(spans + [1]), Xc)
+    W = Xc + 2 * HL
+    hm = max(HL + 1, min(2 * max(spans + [1]), Xc))
     total = sum(max(1, -(-2 * s // Xc)) for s in spans) or 1
-    rows = max(W, Xc + 2, C * Xc) * Z
+    rows = max(Xc + 2, C * Xc) * Z
     R = len(spans)
     dma = pltpu.SemaphoreType.DMA
     scratch = [
@@ -460,25 +467,26 @@
         pltpu.VMEM((C, X + 4, Z, Y), f32), wide, pltpu.VMEM((C, X + 2, Z, Y), f32),
         wide, wide, wide, wide, wide, wide, wide, wide, wide, wide, wide,
         pltpu.VMEM((rows, Y), f32), pltpu.VMEM((rows, Yc), f32),
-        pltpu.VMEM((Xc + 2 * HC, Zc, Yc), f32), pltpu.VMEM((7, W, Zc, Yc), f32),
+        pltpu.VMEM((C, X, Z, Y), f32), pltpu.VMEM((CYCLES, W, Zc, Yc), f32), pltpu.VMEM((7, W, Zc, Yc), f32),
         pltpu.VMEM((C, Xc, Zc, Yc), f32), pltpu.VMEM((Xc + 2 * hm, Zc, Yc), f32),
         pltpu.VMEM((C, Xc + 4, Zc, Yc), f32), pltpu.VMEM((R + 1, C, Xc, Zc, Yc), f32),
         pltpu.VMEM((total, C, Xc + 2 * hm, Zc, Yc), f32),
         pltpu.VMEM((Y, Yc), jnp.bfloat16), pltpu.VMEM((Yc, Y), jnp.bfloat16),
         dma((2,)), dma((2, C)), dma((2, C)), dma((2, 1)), dma((2, 1)), dma((2, 1)), dma((2, 1)),
         dma((2, 1)), dma((2, 1)), dma((2, 1)), dma((2, 1)), dma((2, 1)), dma((2, 1)),
+        dma((CYCLES, 2, 1)), dma((CYCLES, 2, 1)),
         dma((max(R, 1), C)), dma((max(R, 1), C)), dma((total, C, 2, 1)), dma((total, C, 2, 1)),
     ]
     result = pl.pallas_call(
         functools.partial(kernel, n, ntm, spans),
-        out_shape=jax.ShapeDtypeStruct((C, X, Z, Y), f32),
+        out_shape=jax.ShapeDtypeStruct((C, Z, X, Y), f32),
         in_specs=[pl.BlockSpec(memory_space=pltpu.HBM)] * 2,
         out_specs=pl.BlockSpec(memory_space=pltpu.VMEM),
         scratch_shapes=scratch,
         compiler_params=pltpu.CompilerParams(
             collective_id=0, has_side_effects=True, vmem_limit_bytes=60 * 1024 * 1024),
     )(start_states[0], labels)
-    return jnp.swapaxes(result, 1, 2)[None]
+    return result[None]
 
 
 def solution(mesh):

time: 42.5 us -> 43.8 us (1.031)
  Pallas kernels: 39.6 us -> 41.4 us
    broadcast_in_dim x1 -> x0, local copies, waits for them, and re-layouts: 2.47 us -> none  [body(): return jnp.swapaxes(result, 1, 2)[None]]
    unnamed x0 -> x1, local copies, waits for them, and re-layouts: none -> 2.06 us
    pallas_call x1, Pallas kernels: 39.6 us -> 41.4 us  [body(): pl.pallas_call(functools.partial(kernel, n, ntm, spans), out_shape=jax.Sh...]
where the time goes in v4:
time: 43.8 us; the launch traced here: 43.5 us
  Pallas kernels  41.4 us (95%)
  local copies, waits for them, and re-layouts  2.06 us (5%)
    pallas_call x1, Pallas kernels, body(): pl.pallas_call(functools.partial(kernel, n, ntm, spans), out_shape=jax.Sh...  41.4 us
    unnamed x1, local copies, waits for them, and re-layouts  2.06 us

profile of v4, /device:TPU:25, one launch (start us, length us, event | category | flops | bytes accessed | tf_op | source)
XLA Modules:
  0.0 43.5 jit_solution(183749039633361747)
XLA Ops:
  0.0 41.4 %shard_map.28 = f32[3,16,16,256]{3,2,1,0:T(8,128)} custom-call(f32[3,16,16,256]{3,2,1,0:T(8,128)} %bitcast.3, s32[16,16,256]{2,1,0:T(8,128)} %l_in.1), custom_call_target="tpu_custom_call" | custom-call | tf_op jit(solution)/shard_map/pallas_call | solution.py:480
  41.4 2.1 %copy.4 = f32[1,3,16,16,256]{4,3,2,1,0:T(8,128)} copy(f32[1,3,16,16,256]{4,3,2,1,0:T(8,128)} %bitcast.2) | data formatting | bytes 1572864

commit v5 on v3

--- a/solution.py
+++ b/solution.py
@@ -74,7 +74,7 @@
 
 def kernel(n, ntm, spans, u_in, l_in, out, u_raw, l_raw, u, m, pr, t, pa, pb, pc, rd, dg, wx, wzu, wzl, wyu, wyl,
            rs, rz, mc, cw, ce, mcw, csw, part, vb, down, dup,
-           local_sem, us, ur, ms, mr, ts, tr, ps, pr_sem, mcs, mcr, css, csr, ss, sr, fs, fr):
+           local_sem, us, ur, ms, mr, ts, tr, ps, pr_sem, mcs, mcr, css, csr, ss, sr, fs, fr, hs, hr):
     me, tm = lax.axis_index("space"), lax.axis_index("tm")
     Z, X, Y = u_in.shape[1:]
     Xc, Zc, Yc = X // 2, Z // 2, Y // 2
@@ -112,6 +112,17 @@
             pl.semaphore_signal(barrier, inc=1, device_id={"tm": tm + s}, device_id_type=MESH)
 
         count = count + jnp.where(tm >= s, 1, 0) + jnp.where(tm + s < ntm, 1, 0)
+        if 4 * s <= Xc:
+            for by, there in ((-s, tm >= s), (s, tm + s < ntm)):
+                for side, beside in ((-1, has_left), (1, has_right)):
+                    both = jnp.logical_and(there, beside)
+
+                    @pl.when(both)
+                    def _():
+                        pl.semaphore_signal(
+                            barrier, inc=1, device_id={"tm": tm + by, "space": me + side}, device_id_type=MESH)
+
+                    count = count + jnp.where(both, 1, 0)
 
     @pl.when(jnp.logical_not(has_left))
     def _():
@@ -343,7 +354,8 @@
             length = v.shape[0] - 2
             off = (Xc + 2 * hm - length) // 2
             mid = v[1:-1]
-            zu, zl, yu, yl = masked_shifts(mid, edge_masks(mid.shape, 1, 2), 1, 2)
+            inner = [jnp.where(k, 1.0, 0.0) for k in edge_masks((1, Zc, Yc), 1, 2)]
+            zu, zl, yu, yl = [a * b for a, b in zip(shifts(mid, 1, 2), inner)]
             s = v[2:] + v[:-2] + (zu + zl) + (yu + yl)
             v = mid + (RATE * mcw[off:off + length]) * (s - 6.0 * mid)
         return v
@@ -395,10 +407,28 @@
         return Exchange([(lambda f, w: vb.at[k, d, pl.ds(f, w)], hm, 2 * spans[r] // stages[r])],
                         fs.at[k, d], fr.at[k, d], Xc)
 
+    direct = [4 * s <= Xc for s in spans]
+
+    def halo(r, side, target):
+        h, k = 2 * spans[r], starts[r]
+        src, dst = ((0, hm + Xc), (Xc - h, hm - h))[side]
+        return pltpu.make_async_remote_copy(
+            part.at[r, :, pl.ds(src, h)], vb.at[k, :, pl.ds(dst, h)], hs.at[r, side], hr.at[r, side],
+            device_id={"tm": target, "space": me + (-1, 1)[side]}, device_id_type=MESH)
+
+    def send_halo(r):
+        if r < R and direct[r]:
+            s = spans[r]
+            for side, beside in enumerate((has_left, has_right)):
+                @pl.when(jnp.logical_and(tm + s < ntm, beside))
+                def _():
+                    halo(r, side, tm + s).start()
+
     def advance(r, d):
         times = spans[r] // stages[r]
         for q in range(stages[r]):
-            sides(r, q, d).wait()
+            if not direct[r]:
+                sides(r, q, d).wait()
             v = coarse_steps(vb[starts[r] + q, d, hm - 2 * times:hm + Xc + 2 * times], times)
             if q + 1 < stages[r]:
                 vb[starts[r] + q + 1, d, hm:hm + Xc] = v
@@ -409,21 +439,33 @@
     for d in range(C):
         part[0, d] = ce[d] - part[0, d]
         send(0, d)
+    send_halo(0)
     for r, s in enumerate(spans):
         @pl.when(tm < s)
         def _():
             for d in range(C):
                 part[r + 1, d] = part[r, d]
                 send(r + 1, d)
+            send_halo(r + 1)
 
         @pl.when(tm >= s)
         def _():
-            for d in range(C):
-                hop(r, d, tm).wait_recv()
-                sides(r, 0, d).start()
-                if d > 0:
-                    advance(r, d - 1)
-            advance(r, C - 1)
+            if direct[r]:
+                for side, beside in enumerate((has_right, has_left)):
+                    @pl.when(beside)
+                    def _():
+                        halo(r, side, tm).wait_recv()
+
+                for d in range(C):
+                    hop(r, d, tm).wait_recv()
+                    advance(r, d)
+            else:
+                for d in range(C):
+                    hop(r, d, tm).wait_recv()
+                    sides(r, 0, d).start()
+                for d in range(C):
+                    advance(r, d)
+            send_halo(r + 1)
 
     prolonged((part[R] - ce[...]).reshape(C * Xc, Zc, Yc))
     for d in range(C):
@@ -439,6 +481,11 @@
         def _():
             for d in range(C):
                 hop(r, d, tm + s).wait_send()
+        if direct[r]:
+            for side, beside in enumerate((has_left, has_right)):
+                @pl.when(jnp.logical_and(tm + s < ntm, beside))
+                def _():
+                    halo(r, side, tm + s).wait_send()
 
 
 def body(n, ntm, start_states, labels):
@@ -468,6 +515,7 @@
         dma((2,)), dma((2, C)), dma((2, C)), dma((2, 1)), dma((2, 1)), dma((2, 1)), dma((2, 1)),
         dma((2, 1)), dma((2, 1)), dma((2, 1)), dma((2, 1)), dma((2, 1)), dma((2, 1)),
         dma((max(R, 1), C)), dma((max(R, 1), C)), dma((total, C, 2, 1)), dma((total, C, 2, 1)),
+        dma((max(R, 1), 2)), dma((max(R, 1), 2)),
     ]
     result = pl.pallas_call(
         functools.partial(kernel, n, ntm, spans),

time: 42.5 us -> 39 us (0.918)
  Pallas kernels: 39.6 us -> 36.3 us
    pallas_call x1, Pallas kernels: 39.6 us -> 36.3 us  [body(): pl.pallas_call(functools.partial(kernel, n, ntm, spans), out_shape=jax.Sh...]
where the time goes in v5:
time: 39 us; the launch traced here: 38.8 us
  Pallas kernels  36.3 us (93%)
  local copies, waits for them, and re-layouts  2.47 us (6%)
    pallas_call x1, Pallas kernels, body(): pl.pallas_call(functools.partial(kernel, n, ntm, spans), out_shape=jax.Sh...  36.3 us
    broadcast_in_dim x1, local copies, waits for them, and re-layouts, body(): return jnp.swapaxes(result, 1, 2)[None]  2.47 us

profile of v5, /device:TPU:25, one launch (start us, length us, event | category | flops | bytes accessed | tf_op | source)
XLA Modules:
  0.0 38.8 jit_solution(10985532492699391704)
XLA Ops:
  0.0 36.3 %shard_map.28 = f32[3,16,16,256]{3,2,1,0:T(8,128)} custom-call(f32[3,16,16,256]{3,2,1,0:T(8,128)} %bitcast.5, s32[16,16,256]{2,1,0:T(8,128)} %l_in.1), custom_call_target="tpu_custom_call" | custom-call | tf_op jit(solution)/shard_map/pallas_call | solution.py:520
  36.3 2.5 %copy.3 = f32[1,3,16,16,256]{4,3,2,1,0:T(8,128)} copy(f32[1,3,16,16,256]{4,2,3,1,0:T(8,128)} %bitcast.4) | data formatting | bytes 1572864 | tf_op jit(solution)/shard_map/broadcast_in_dim | solution.py:529

commit v6 on v5

--- a/solution.py
+++ b/solution.py
@@ -229,6 +229,38 @@
     u_x.start()
     m_x.start()
 
+    fine_masks = edge_masks((Z, Y), 0, 1)
+
+    def lap(d, i):
+        v = u[d, i]
+        summed = u[d, i - 1] + u[d, i + 1]
+        zu, zl, yu, yl = masked_shifts(v, fine_masks, 0, 1)
+        summed = summed + (zu + zl) + (yu + yl)
+        return v + VISCOSITY * (summed - 6.0 * v)
+
+    def predict(i):
+        pr[0, i] = lap(0, i + 1) + BUOYANCY * (2.0 * m[i - 1 + H] - 1.0)
+        pr[1, i] = lap(1, i + 1)
+        pr[2, i] = lap(2, i + 1)
+
+    planes(2, X, predict, 7)
+
+    def aim(i):
+        zu, zl, _, _ = masked_shifts(pr[0, i], fine_masks, 0, 1)
+        _, _, yu, yl = masked_shifts(pr[2, i], fine_masks, 0, 1)
+        t[i - 1 + H] = -0.5 * ((zu - zl) + (pr[1, i + 1] - pr[1, i - 1]) + (yu - yl))
+
+    planes(3, X - 1, aim, 6)
+    u_x.wait()
+    predict(1)
+    predict(X)
+    pr[1, 0] = jnp.where(has_left, lap(1, 1), 0.0)
+    pr[1, X + 1] = jnp.where(has_right, lap(1, X + 2), 0.0)
+
+    for i in (1, 2, X - 1, X):
+        aim(i)
+    t_x.start()
+
     mine = restricted(Xc, lambda j: m[H + 2 * j] + m[H + 2 * j + 1])
     mc[HC:HC + Xc] = mine
     mcw[hm:hm + Xc] = mine
@@ -237,34 +269,6 @@
     csw[:, 2:2 + Xc] = averaged(C * Xc).reshape(C, Xc, Zc, Yc)
     mc_x = Exchange([(plane_view(mcw), hm, hm)], mcs, mcr, Xc)
     cs_x = Exchange([(lambda f, w: csw.at[:, pl.ds(f, w)], 2, 2)], css, csr, Xc)
-
-    fine_masks = edge_masks((Z, Y), 0, 1)
-
-    def lap(d, i):
-        v = u[d, i]
-        summed = u[d, i - 1] + u[d, i + 1]
-        zu, zl, yu, yl = masked_shifts(v, fine_masks, 0, 1)
-        summed = summed + (zu + zl) + (yu + yl)
-        return v + VISCOSITY * (summed - 6.0 * v)
-
-    u_x.wait()
-
-    def predict(i):
-        pr[0, i] = lap(0, i + 1) + BUOYANCY * (2.0 * m[i - 1 + H] - 1.0)
-        pr[1, i] = lap(1, i + 1)
-        pr[2, i] = lap(2, i + 1)
-
-    planes(1, X + 1, predict)
-    pr[1, 0] = jnp.where(has_left, lap(1, 1), 0.0)
-    pr[1, X + 1] = jnp.where(has_right, lap(1, X + 2), 0.0)
-
-    def aim(i):
-        zu, zl, _, _ = masked_shifts(pr[0, i], fine_masks, 0, 1)
-        _, _, yu, yl = masked_shifts(pr[2, i], fine_masks, 0, 1)
-        t[i - 1 + H] = -0.5 * ((zu - zl) + (pr[1, i + 1] - pr[1, i - 1]) + (yu - yl))
-
-    planes(1, X + 1, aim)
-    t_x.start()
 
     m_x.wait()
 

time: 39 us -> 38.4 us (0.985)
  Pallas kernels: 36.3 us -> 35.7 us
    pallas_call x1, Pallas kernels: 36.3 us -> 35.7 us  [body(): pl.pallas_call(functools.partial(kernel, n, ntm, spans), out_shape=jax.Sh...]
where the time goes in v6:
time: 38.4 us; the launch traced here: 38.2 us
  Pallas kernels  35.7 us (93%)
  local copies, waits for them, and re-layouts  2.47 us (6%)
    pallas_call x1, Pallas kernels, body(): pl.pallas_call(functools.partial(kernel, n, ntm, spans), out_shape=jax.Sh...  35.7 us
    broadcast_in_dim x1, local copies, waits for them, and re-layouts, body(): return jnp.swapaxes(result, 1, 2)[None]  2.47 us

profile of v6, /device:TPU:25, one launch (start us, length us, event | category | flops | bytes accessed | tf_op | source)
XLA Modules:
  0.0 38.2 jit_solution(11396786555851466895)
XLA Ops:
  0.0 35.7 %shard_map.28 = f32[3,16,16,256]{3,2,1,0:T(8,128)} custom-call(f32[3,16,16,256]{3,2,1,0:T(8,128)} %bitcast.5, s32[16,16,256]{2,1,0:T(8,128)} %l_in.1), custom_call_target="tpu_custom_call" | custom-call | tf_op jit(solution)/shard_map/pallas_call | solution.py:524
  35.7 2.5 %copy.3 = f32[1,3,16,16,256]{4,3,2,1,0:T(8,128)} copy(f32[1,3,16,16,256]{4,2,3,1,0:T(8,128)} %bitcast.4) | data formatting | bytes 1572864 | tf_op jit(solution)/shard_map/broadcast_in_dim | solution.py:533

commit v7 on v6

--- a/solution.py
+++ b/solution.py
@@ -376,20 +376,6 @@
     coarse_correct(pa)
     smooth(pa, pc, H - 1, H + X + 1)
 
-    def finish(i):
-        v = pc[i]
-        zu, zl, yu, yl = masked_shifts(v, fine_masks, 0, 1)
-        k = i - H + 1
-        half = 0.5 * m[i]
-        out[0, i - H] = pr[0, k] - half * (zu - zl)
-        out[1, i - H] = pr[1, k] - half * (pc[i + 1] - pc[i - 1])
-        out[2, i - H] = pr[2, k] - half * (yu - yl)
-
-    planes(H, H + X, finish)
-    for d in range(C):
-        fill(0, Xc, lambda j: out[d, 2 * j] + out[d, 2 * j + 1], d * Xc)
-    ce[...] = averaged(C * Xc).reshape(C, Xc, Zc, Yc)
-
     stages, starts = [], []
     for s in spans:
         starts.append(sum(stages))
@@ -440,7 +426,18 @@
         part[r + 1, d] = part[r, d] + v
         send(r + 1, d)
 
+    def finish(d, i):
+        if d == 1:
+            grad = pc[i + 1] - pc[i - 1]
+        else:
+            zu, zl, yu, yl = masked_shifts(pc[i], fine_masks, 0, 1)
+            grad = zu - zl if d == 0 else yu - yl
+        out[d, i - H] = pr[d, i - H + 1] - 0.5 * m[i] * grad
+
     for d in range(C):
+        planes(H, H + X, lambda i: finish(d, i))
+        fill(0, Xc, lambda j: out[d, 2 * j] + out[d, 2 * j + 1])
+        ce[d] = averaged(Xc)
         part[0, d] = ce[d] - part[0, d]
         send(0, d)
     send_halo(0)

time: 38.4 us -> 38.1 us (level)
  no operation moved by 1% of the time
where the time goes in v7:
time: 38.1 us; the launch traced here: 37.9 us
  Pallas kernels  35.4 us (93%)
  local copies, waits for them, and re-layouts  2.47 us (6%)
    pallas_call x1, Pallas kernels, body(): pl.pallas_call(functools.partial(kernel, n, ntm, spans), out_shape=jax.Sh...  35.4 us
    broadcast_in_dim x1, local copies, waits for them, and re-layouts, body(): return jnp.swapaxes(result, 1, 2)[None]  2.47 us

profile of v7, /device:TPU:25, one launch (start us, length us, event | category | flops | bytes accessed | tf_op | source)
XLA Modules:
  0.0 37.9 jit_solution(8328021136681339058)
XLA Ops:
  0.0 35.4 %shard_map.28 = f32[3,16,16,256]{3,2,1,0:T(8,128)} custom-call(f32[3,16,16,256]{3,2,1,0:T(8,128)} %bitcast.5, s32[16,16,256]{2,1,0:T(8,128)} %l_in.1), custom_call_target="tpu_custom_call" | custom-call | tf_op jit(solution)/shard_map/pallas_call | solution.py:521
  35.4 2.5 %copy.3 = f32[1,3,16,16,256]{4,3,2,1,0:T(8,128)} copy(f32[1,3,16,16,256]{4,2,3,1,0:T(8,128)} %bitcast.4) | data formatting | bytes 1572864 | tf_op jit(solution)/shard_map/broadcast_in_dim | solution.py:530
